TPU v7x, 256 devices: a whole 4x4x8 slice. The times are simulated.
256 devices in a mesh: src: 8 (over z), tgt: 32 (over y, x, core).
Axes of the slice: x: 4, y: 4, z: 8, core: 2. Of those that a mesh axis runs over, the one named last changes fastest.
Arguments:
- src_feat: float32 [16, 32768], P(None, ('src', 'tgt')), may hold values from -1.5 to 16
- tgt_feat: float32 [16, 32768], P(None, ('tgt', 'src')), may hold values from -1.5 to 1.5
- src_mass: float32 [32768], P(('src', 'tgt')), may hold values from 0.2 to 6
- tgt_mass: float32 [32768], P(('tgt', 'src')), may hold values from 0.2 to 6
- g_init: float32 [32768], P('tgt'), may hold values from -3 to 3
Outputs:
- source_potential: float32 [32768], P(('src', 'tgt'))
- target_potential: float32 [32768], P('tgt')
- bary_map: float32 [16, 32768], P(None, ('src', 'tgt'))
All inputs are finite; a program needn't handle non-finite values.
Results may differ from a plain program's by a relative error of at most 0.0003.
Values sent between devices are 32-bit elements; how exact they have to be, the bound alone decides.
No kernel may reach another device: no remote copies, remote signals or barrier semaphores. Data moves between devices by JAX's collectives and lax.ppermute only.
A program may use at most 64 MiB of HBM per device.

v0:
```python
import math

import jax
import jax.numpy as jnp
from jax import lax
from jax.sharding import PartitionSpec as P

epsilon = 0.5


def cost_block(block, others):
    cross = jnp.einsum("fi,fj->ij", block, others, precision=lax.Precision.HIGHEST)
    return jnp.sum(block * block, 0)[:, None] + jnp.sum(others * others, 0)[None, :] - 2.0 * cross


def split_blocks(feats):
    width, count = feats.shape
    size = math.gcd(count, 512)
    return feats.reshape(width, count // size, size).transpose(1, 0, 2)


def partial_lse(feats, others, potential):

    def partial_one_block(block):
        scores = (potential[None, :] - cost_block(block, others)) / epsilon
        top = jnp.max(scores, 1)
        return (top, jnp.sum(jnp.exp(scores - top[:, None]), 1))

    tops, totals = lax.map(partial_one_block, split_blocks(feats))
    return (tops.reshape(feats.shape[1]), totals.reshape(feats.shape[1]))


def rows_total(local_top, local_sum):
    top = lax.pmax(local_top, "tgt")
    total = lax.psum(local_sum * jnp.exp(local_top - top), "tgt")
    return top + jnp.log(total)


def cols_total(local_top, local_sum):
    top = lax.pmax(local_top, "src")
    total = lax.psum(local_sum * jnp.exp(local_top - top), "src")
    return top + jnp.log(total)


def local(src_feat, tgt_feat, src_mass, tgt_mass, g_init):
    totals = lax.psum((jnp.sum(src_mass), jnp.sum(tgt_mass)), ("src", "tgt"))
    rows_feat, rows_mass = (
        lax.all_gather(src_feat, "tgt", axis=1, tiled=True),
        lax.all_gather(src_mass, "tgt", axis=0, tiled=True),
    )
    cols_feat, cols_mass = (
        lax.all_gather(tgt_feat, "src", axis=1, tiled=True),
        lax.all_gather(tgt_mass, "src", axis=0, tiled=True),
    )
    log_a = jnp.log(rows_mass / totals[0])
    log_b = jnp.log(cols_mass / totals[1])
    first_f = epsilon * log_a - epsilon * rows_total(*partial_lse(rows_feat, cols_feat, g_init))
    target_potential = epsilon * log_b - epsilon * cols_total(
        *partial_lse(cols_feat, rows_feat, first_f)
    )
    count = src_feat.shape[1]
    offset = lax.axis_index("tgt") * count
    potential = epsilon * log_a - epsilon * rows_total(
        *partial_lse(rows_feat, cols_feat, target_potential)
    )
    size = math.gcd(rows_feat.shape[1], 512)
    pot_blocks = potential.reshape(-1, size)
    mass_blocks = log_a.reshape(-1, size)

    def body_one_block(items):
        block, pot_rows, mass_rows = items
        weights = jnp.exp(
            (pot_rows[:, None] + target_potential[None, :] - cost_block(block, cols_feat)) / epsilon
            - mass_rows[:, None]
        )
        return jnp.einsum("ij,fj->fi", weights, cols_feat, precision=lax.Precision.HIGHEST)

    sums = lax.map(body_one_block, (split_blocks(rows_feat), pot_blocks, mass_blocks))
    numer = sums.transpose(1, 0, 2).reshape(rows_feat.shape[0], rows_feat.shape[1])
    bary_map = lax.psum_scatter(numer, "tgt", scatter_dimension=1, tiled=True)
    source_potential = lax.dynamic_slice_in_dim(potential, offset, count, 0)
    return (source_potential, target_potential, bary_map)


def solution(mesh):
    placed = (
        P(None, ("src", "tgt")),
        P(None, ("tgt", "src")),
        P(("src", "tgt")),
        P(("tgt", "src")),
        P("tgt"),
    )
    return jax.shard_map(
        local,
        mesh=mesh,
        in_specs=placed,
        out_specs=(P(("src", "tgt")), P("tgt"), P(None, ("src", "tgt"))),
        check_vma=False,
    )
```

profile of v0, /device:TPU:1, one launch (start us, length us, event | category | flops | bytes accessed | tf_op | source)
XLA Modules:
  0.0 891.1 jit_solution(18202135094398825574)
XLA Ops:
  7.2 23.1 %all_gather.15 = f32[16,1024]{1,0:T(8,128)S(1)} all-gather(f32[16,128]{1,0:T(8,128)} %param.14), channel_id=1, replica_groups=mesh['src'=8,'tgt'=32] {'src'}, dimensions={1}, use_global_device_ids=true | all-gather | bytes 73728 | tf_op jit(solution)/shard_map/all_gather | solution.py:52
  30.4 31.6 %all_gather.14 = f32[16,4096]{1,0:T(8,128)S(1)} all-gather(f32[16,128]{1,0:T(8,128)} %param.13), channel_id=1, replica_groups=mesh['src'=8,'tgt'=32] {'tgt'}, dimensions={1}, use_global_device_ids=true | all-gather | bytes 270336 | tf_op jit(solution)/shard_map/all_gather | solution.py:48
  62.4 29.5 %while.54 = (s32[]{:T(128)}, f32[8,512]{1,0:T(8,128)S(1)}, f32[8,512]{1,0:T(8,128)S(1)}, f32[1024]{0:T(1024)}, f32[8,16,512]{2,1,0:T(8,128)S(1)}, /*index=5*/f32...) while((s32[]{:T(128)}, f32[8,512]{1,0:T(8,128)S(1)}, f32[8,512]{1,0:T(8,128)S(1)}, ...), condition=%wide.region_9.10_spmd, body=%wide.region_5.9_spmd.sunk | while | flops 104872448 | bytes 4352109 | solution.py:29
  62.4 3.0 fusion.66
  66.1 3.0 fusion.66
  69.8 3.0 fusion.66
  73.5 3.0 fusion.66
  80.8 3.0 fusion.66
  88.2 3.0 fusion.66
  91.9 120.8 %pmax.21 = f32[4096]{0:T(1024)S(1)} all-reduce(f32[4096]{0:T(1024)S(1)} %bitcast.135), channel_id=1, replica_groups=mesh['src'=8,'tgt'=32] {'tgt'}, use_global_device_ids=true, to_apply=%region_10.11 | all-reduce | flops 4096 | bytes 32768 | tf_op jit(solution)/shard_map/pmax | solution.py:34
  212.7 123.8 %psum.37 = f32[4096]{0:T(1024)S(1)} all-reduce(f32[4096]{0:T(1024)S(1)} %exponential_multiply_fusion.1), channel_id=1, replica_groups=mesh['src'=8,'tgt'=32] {'tgt'}, use_global_device_ids=true, to_apply=%region_11.12 | all-reduce | flops 4096 | bytes 32768 | tf_op jit(solution)/shard_map/psum | solution.py:35
  337.1 22.8 %all-gather = f32[32,1,128]{2,1,0:T(1,128)S(1)} all-gather(f32[1,1,128]{2,1,0:T(1,128)S(1)} %bitcast.155), channel_id=1, replica_groups=mesh['src'=8,'tgt'=32] {'tgt'}, dimensions={0}, use_global_device_ids=true | all-gather | bytes 16896 | tf_op jit(solution)/shard_map/all_gather | solution.py:49
  360.5 75.6 %all-reduce = (f32[]{:T(128)}, f32[]{:T(128)}) all-reduce(f32[]{:T(128)} %reduce_sum.129, f32[]{:T(128)} %reduce_sum.130), channel_id=1, replica_groups=mesh['src'=8,'tgt'=32] {'src','tgt'}, use_global_device_ids=true, to_apply=%region_1.0 | all-reduce | flops 2 | bytes 16 | tf_op jit(solution)/shard_map/psum | solution.py:46
  438.1 19.2 %while.55 = (s32[]{:T(128)}, f32[2,512]{1,0:T(2,128)S(1)}, f32[2,512]{1,0:T(2,128)S(1)}, f32[4096]{0:T(1024)S(1)}, f32[2,16,512]{2,1,0:T(8,128)S(1)}, /*index=5*...) while((s32[]{:T(128)}, f32[2,512]{1,0:T(2,128)S(1)}, f32[2,512]{1,0:T(2,128)S(1)}, ...), condition=%wide.region_17.18_spmd, body=%wide.region_13.17_spmd.sunk | while | flops 419445248 | bytes 17156204 | solution.py:29
  438.1 8.2 fusion.69
  447.7 8.2 fusion.69
  457.3 11.4 %pmax.22 = f32[1024]{0:T(1024)S(1)} all-reduce(f32[1024]{0:T(1024)S(1)} %bitcast.149), channel_id=1, replica_groups=mesh['src'=8,'tgt'=32] {'src'}, use_global_device_ids=true, to_apply=%region_18.19 | all-reduce | flops 1024 | bytes 8192 | tf_op jit(solution)/shard_map/pmax | solution.py:40
  468.7 12.0 %psum.38 = f32[1024]{0:T(1024)S(1)} all-reduce(f32[1024]{0:T(1024)S(1)} %exponential_multiply_fusion.2), channel_id=1, replica_groups=mesh['src'=8,'tgt'=32] {'src'}, use_global_device_ids=true, to_apply=%region_19.20 | all-reduce | flops 1024 | bytes 8192 | tf_op jit(solution)/shard_map/psum | solution.py:41
  480.7 10.6 %all-gather.1 = f32[8,1,128]{2,1,0:T(1,128)S(1)} all-gather(f32[1,1,128]{2,1,0:T(1,128)S(1)} %bitcast.156), channel_id=1, replica_groups=mesh['src'=8,'tgt'=32] {'src'}, dimensions={0}, use_global_device_ids=true | all-gather | bytes 4608 | tf_op jit(solution)/shard_map/all_gather | solution.py:53
  492.0 24.1 %while.56 = (s32[]{:T(128)}, f32[8,512]{1,0:T(8,128)S(1)}, f32[8,512]{1,0:T(8,128)S(1)}, f32[1024]{0:T(1024)S(1)}, f32[8,16,512]{2,1,0:T(8,128)S(1)}, /*index=5*...) while((s32[]{:T(128)}, f32[8,512]{1,0:T(8,128)S(1)}, f32[8,512]{1,0:T(8,128)S(1)}, ...), condition=%wide.region_24.25_spmd, body=%wide.region_20.24_spmd.sunk | while | flops 104872448 | bytes 4352109 | solution.py:29
  516.0 129.6 %pmax.23 = f32[4096]{0:T(1024)S(1)} all-reduce(f32[4096]{0:T(1024)S(1)} %bitcast.137), channel_id=1, replica_groups=mesh['src'=8,'tgt'=32] {'tgt'}, use_global_device_ids=true, to_apply=%region_25.26 | all-reduce | flops 4096 | bytes 32768 | tf_op jit(solution)/shard_map/pmax | solution.py:34
  645.6 123.8 %psum.39 = f32[4096]{0:T(1024)S(1)} all-reduce(f32[4096]{0:T(1024)S(1)} %exponential_multiply_fusion), channel_id=1, replica_groups=mesh['src'=8,'tgt'=32] {'tgt'}, use_global_device_ids=true, to_apply=%region_26.27 | all-reduce | flops 4096 | bytes 32768 | tf_op jit(solution)/shard_map/psum | solution.py:35
  769.5 35.7 %while.57 = (s32[]{:T(128)}, f32[8,16,512]{2,1,0:T(8,128)S(1)}, f32[8,512]{1,0:T(8,128)S(1)}, f32[1024]{0:T(1024)S(1)}, f32[8,16,512]{2,1,0:T(8,128)S(1)}, /*ind...) while((s32[]{:T(128)}, f32[8,16,512]{2,1,0:T(8,128)S(1)}, ...), condition=%wide.region_29.30_spmd, body=%wide.region_27.29_spmd.sunk | while | flops 205012480 | bytes 4448365 | solution.py:78
  806.5 77.8 %reduce-scatter.2.cloned.1.call-done = f32[16,128]{1,0:T(8,128)} async-done(((f32[16,4096]{1,0:T(8,128)}), f32[16,128]{1,0:T(8,128)}) %reduce-scatter.2.cloned.1.call-update) | async-done | bytes 8208 | tf_op jit(solution)/shard_map/reduce_scatter | solution.py:80
  (156 shorter events, 79.0 us)
Async XLA Ops:
  7.2 877.1 %reduce-scatter.2.cloned.1.call-start = ((), (), s32[]{:S(2)}) async-start(), calls=%async_computation.1 | async-start | bytes 270336 | tf_op jit(solution)/shard_map/reduce_scatter | solution.py:80
  62.4 274.2 %copy-start.1 = (f32[128]{0:T(128)S(1)}, f32[128]{0:T(128)}, u32[]{:S(2)}) copy-start(f32[128]{0:T(128)} %param.15) | copy-start | bytes 1540
  62.4 297.6 %copy-start.2 = (f32[128]{0:T(128)S(1)}, f32[128]{0:T(128)}, u32[]{:S(2)}) copy-start(f32[128]{0:T(128)} %param.16) | copy-start | bytes 1540
  805.1 79.1 %copy-start = (f32[1024]{0:T(1024)}, f32[1024]{0:T(1024)S(1)}, u32[]{:S(2)}) copy-start(f32[1024]{0:T(1024)S(1)} %get-tuple-element.758) | copy-start | bytes 12292
Sparse Core Ops, SparseCore 0:
  806.0 78.2 reduce-scatter.1
where the time goes:
time: 893 us; the launch traced here: 891 us
  blocking collectives  685 us (77%)
  matrix products  94.1 us (11%)
  waiting for transfers between devices  77.8 us (9%)
  other arithmetic  14.9 us (2%)
  between operations  14.2 us (2%)
    pmax x2, blocking collectives, rows_total(): top = lax.pmax(local_top, 'tgt')  250 us
    psum x2, blocking collectives, rows_total(): total = lax.psum(local_sum * jnp.exp(local_top - top), 'tgt')  248 us
    reduce_scatter x1, waiting for transfers between devices, local(): bary_map = lax.psum_scatter(numer, 'tgt', scatter_dimension=1, tiled=True)  77.8 us
    psum x1, blocking collectives, local(): totals = lax.psum((jnp.sum(src_mass), jnp.sum(tgt_mass)), ('src', 'tgt'))  75.6 us
    dot_general x26, matrix products, cost_block(): jnp.einsum('fi,fj->ij', block, others, precision=lax.Precision.HIGHEST)  73.7 us
    all_gather x1, blocking collectives, local(): lax.all_gather(src_feat, 'tgt', axis=1, tiled=True)  31.6 us
    all_gather x1, blocking collectives, local(): lax.all_gather(tgt_feat, 'src', axis=1, tiled=True)  23.1 us
    all_gather x1, blocking collectives, local(): lax.all_gather(src_mass, 'tgt', axis=0, tiled=True)  22.8 us
  transfers between devices with their start and end apart: 1, of which 1 were waited for; matrix products, arithmetic and copies ran while one was open for 0% of the time, Pallas kernels for 0%

commit v1 on v0

v1 whole, which is shorter than its diff:
```python
import functools

import jax
import jax.numpy as jnp
from jax import lax
from jax.experimental import pallas as pl
from jax.experimental.pallas import tpu as pltpu
from jax.sharding import Mesh, PartitionSpec as P

f32 = jnp.float32
bf16 = jnp.bfloat16
LOG2E = 1.4426950408889634
LN2 = 0.6931471805599453
epsilon = 0.5
UNIT = LOG2E / epsilon

T_ORDER = (0, 0, 1, 0, 1, 2)
S_ORDER = (0, 1, 0, 2, 1, 0)
COLS = ("z", "x")
ROWS = ("y", "c")


def split3(v):
    hi = v.astype(bf16)
    rest = v - hi.astype(f32)
    mid = rest.astype(bf16)
    return hi, mid, (rest - mid.astype(f32)).astype(bf16)


def bias_rows(row):
    hi, mid, lo = (jnp.broadcast_to(p.astype(f32), (16, 128)) for p in split3(row))
    r = lax.broadcasted_iota(jnp.int32, (16, 128), 0)
    return jnp.where(r == 0, hi, jnp.where(r == 1, mid, jnp.where(r == 2, lo, 0.0))).astype(bf16)


def put_feats(aug, k, feats, order):
    pieces = split3(feats)
    for at, which in enumerate(order):
        aug[at * 16 : at * 16 + 16, k * 128 : k * 128 + 128] = pieces[which]


def fill_tgt(aug, tall, bias):
    aug[112:128, :] = jnp.ones((16, aug.shape[1]), bf16)
    for k in range(tall.shape[0]):
        put_feats(aug, k, tall[k, 0:16, :], T_ORDER)
        if bias is not None:
            aug[96:112, k * 128 : k * 128 + 128] = bias_rows(bias(k))
    if bias is None:
        aug[96:112, :] = jnp.zeros((16, aug.shape[1]), bf16)


def fill_src(aug, turned, sall, bias):
    aug[96:112, :] = jnp.ones((16, aug.shape[1]), bf16)
    for k in range(sall.shape[0]):
        put_feats(aug, k, sall[k, 0:16, :] * (2.0 * UNIT), S_ORDER)
        if bias is not None:
            aug[112:128, k * 128 : k * 128 + 128] = bias_rows(bias(k))
    if bias is None:
        aug[112:128, :] = jnp.zeros((16, aug.shape[1]), bf16)
    for k in range(sall.shape[0]):
        turned[k * 128 : k * 128 + 128, :] = aug[:, k * 128 : k * 128 + 128].T


def lse2(parts):
    top = jnp.max(parts, 0)
    return top + jnp.log2(jnp.sum(jnp.exp2(parts - top[None]), 0))


def total(rows):
    return jnp.sum(jnp.sum(rows, 0, keepdims=True), 1, keepdims=True)


def pack_body(zat, src_feat, tgt_feat, src_mass, tgt_mass, g, tmsg, smsg):
    g_own = g[pl.ds(zat[0], 1), :]
    for k in range(tmsg.shape[0]):
        tmsg[k, 0:16, :] = tgt_feat[...]
        tmsg[k, 16:17, :] = g_own
        tmsg[k, 17:18, :] = tgt_mass[...]
        tmsg[k, 18:19, :] = src_mass[...]
    for k in range(smsg.shape[0]):
        smsg[k, 0:16, :] = src_feat[...]
        smsg[k, 16:17, :] = src_mass[...]


def first_body(tall, sall, out, taug, saug, turned):
    def bias(k):
        y = tall[k, 0:16, :]
        return UNIT * (tall[k, 16:17, :] - jnp.sum(y * y, 0, keepdims=True))

    fill_tgt(taug, tall, bias)
    fill_src(saug, turned, sall, None)
    n = out.shape[0]
    for r in range(sall.shape[0]):
        v = lax.dot(turned[r * 128 : r * 128 + 128, :], taug[...], preferred_element_type=f32)
        top = jnp.max(v, 1, keepdims=True)
        s = jnp.sum(jnp.exp2(v - top), 1, keepdims=True)
        line = jnp.broadcast_to(top + jnp.log2(s), (128, 128)).T[0:1, :]
        for d in range(n):
            out[d, r : r + 1, :] = line
    tmass = jnp.sum(tall[:, 17, :], 0, keepdims=True)
    smass = jnp.sum(tall[:, 18, :], 0, keepdims=True)
    for d in range(n):
        out[d, 8:9, :] = smass
        out[d, 9:10, :] = tmass


def second_body(part, tall, sall, out, taug, saug, turned):
    lse = lse2(part[:, 0:8, :])

    def bias(k):
        return jnp.log2(sall[k, 16:17, :]) - lse[k : k + 1, :]

    fill_tgt(taug, tall, None)
    fill_src(saug, turned, sall, bias)
    for c in range(taug.shape[1] // 256):
        v = lax.dot(turned[...], taug[:, c * 256 : c * 256 + 256], preferred_element_type=f32)
        v = v.reshape(v.shape[0] // 8, 8, 256)
        top = jnp.max(v, 0)
        s = jnp.sum(jnp.exp2(v - top[None]), 0)
        most = jnp.max(top, 0, keepdims=True)
        s = jnp.sum(s * jnp.exp2(top - most), 0, keepdims=True)
        line = most + jnp.log2(s)
        for d in range(out.shape[0]):
            out[d, 2 * c : 2 * c + 1, :] = line[:, :128]
            out[d, 2 * c + 1 : 2 * c + 2, :] = line[:, 128:]


def third_body(xat, part, first, tall, sall, out, pot, taug, saug, turned, held):
    held[...] = jnp.log2(tall[:, 17, :]) - lse2(part[...])
    fill_tgt(taug, tall, lambda k: held[k : k + 1, :])
    fill_src(saug, turned, sall, None)
    for r in range(sall.shape[0]):
        v = lax.dot(turned[r * 128 : r * 128 + 128, :], taug[...], preferred_element_type=f32)
        top = jnp.max(v, 1, keepdims=True)
        w = jnp.exp2(v - top)
        hi = w.astype(bf16)
        lo = (w - hi.astype(f32)).astype(bf16)
        dims = (((1,), (1,)), ((), ()))
        acc = lax.dot_general(hi, taug[...], dims, preferred_element_type=f32)
        acc = acc + lax.dot_general(lo, taug[...], dims, preferred_element_type=f32)
        acc = acc.T
        s = acc[112:113, :]
        out[r, 0:16, :] = (acc[0:16, :] + acc[32:48, :] + acc[80:96, :]) / s
        out[r, 16:17, :] = jnp.broadcast_to(top, (128, 128)).T[0:1, :] + jnp.log2(s)
    shift = jnp.log2(total(first[:, 8, :])) - jnp.log2(total(first[:, 9, :]))
    for z in range(pot.shape[0]):
        at = 4 * z + xat[0]
        y = tall[pl.ds(at, 1), 0:16, :][0]
        pot[z : z + 1, :] = (held[pl.ds(at, 1), :] + shift) / UNIT + jnp.sum(y * y, 0, keepdims=True)


def last_body(part, first, feat, mass, pot, bary):
    lses = part[:, 16, :]
    top = jnp.max(lses, 0, keepdims=True)
    w = jnp.exp2(lses - top)
    s = jnp.sum(w, 0, keepdims=True)
    acc = jnp.zeros((16, 128), f32)
    for k in range(part.shape[0]):
        acc = acc + part[k, 0:16, :] * w[k : k + 1, :]
    bary[...] = acc / s
    shift = jnp.log2(total(first[:, 9, :])) - 2.0 * jnp.log2(total(first[:, 8, :]))
    x = feat[...]
    lse = top + jnp.log2(s)
    pot[...] = (jnp.log2(mass[...]) - lse + shift) / UNIT + jnp.sum(x * x, 0, keepdims=True)


def call(body, outs, args, scratch=(), scalars=0):
    vmem = pl.BlockSpec(memory_space=pltpu.VMEM)
    smem = pl.BlockSpec(memory_space=pltpu.SMEM)
    return pl.pallas_call(
        body,
        out_shape=[jax.ShapeDtypeStruct(s, f32) for s in outs],
        in_specs=[smem] * scalars + [vmem] * (len(args) - scalars),
        out_specs=[vmem] * len(outs),
        scratch_shapes=list(scratch),
        compiler_params=pltpu.CompilerParams(vmem_limit_bytes=48 << 20),
    )(*args)


def exchange(v, axes):
    return lax.all_to_all(v, axes, 0, 0, tiled=True)


def local(src_feat, tgt_feat, src_mass, tgt_mass, g_init):
    zat = lax.axis_index("z").reshape(1)
    xat = lax.axis_index("x").reshape(1)
    smass = src_mass.reshape(1, 128)
    nt, ns = 32, 8
    aug = [pltpu.VMEM((128, nt * 128), bf16), pltpu.VMEM((128, ns * 128), bf16), pltpu.VMEM((ns * 128, 128), bf16)]
    tmsg, smsg = call(
        pack_body,
        [(nt, 19, 128), (ns, 17, 128)],
        (zat, src_feat, tgt_feat, smass, tgt_mass.reshape(1, 128), g_init.reshape(8, 128)),
        scalars=1,
    )
    tall = exchange(tmsg, COLS)
    sall = exchange(smsg, ROWS)
    (msg,) = call(first_body, [(ns, 10, 128)], (tall, sall), aug)
    first = exchange(msg, ROWS)
    (msg,) = call(second_body, [(nt, nt, 128)], (first, tall, sall), aug)
    second = exchange(msg, COLS)
    msg, tgt_pot = call(
        third_body,
        [(ns, 17, 128), (8, 128)],
        (xat, second, first, tall, sall),
        aug + [pltpu.VMEM((nt, 128), f32)],
        scalars=1,
    )
    third = exchange(msg, ROWS)
    src_pot, bary = call(last_body, [(1, 128), (16, 128)], (third, first, src_feat, smass))
    return src_pot.reshape(128), tgt_pot.reshape(1024), bary


def solution(mesh):
    axes = ("z", "y", "x", "c")
    split = Mesh(mesh.devices.reshape(8, 4, 4, 2), axes)
    src, tgt = ("z", "y", "x", "c"), ("y", "x", "c", "z")
    return jax.shard_map(
        local,
        mesh=split,
        in_specs=(P(None, src), P(None, tgt), P(src), P(tgt), P(("y", "x", "c"))),
        out_specs=(P(src), P(("y", "x", "c")), P(None, src)),
        check_vma=False,
    )
```

time: 893 us -> 97.2 us (0.11)
  blocking collectives: 685 us -> 55.5 us
  matrix products: 94.1 us -> 0 us
  waiting for transfers between devices: 77.8 us -> 15.5 us
  Pallas kernels: 0 us -> 19.6 us
  other arithmetic: 14.9 us -> 0 us
  between operations: 14.2 us -> 0.69 us
    psum x4 -> x0, blocking collectives: 335 us -> none  [the longest x2 248 us: rows_total(): total = lax.psum(local_sum * jnp.exp(local_top - top), 'tgt')]
    pmax x3 -> x0, blocking collectives: 262 us -> none  [the longest x2 250 us: rows_total(): top = lax.pmax(local_top, 'tgt')]
    dot_general x34 -> x0, matrix products: 94.1 us -> none  [the longest x26 73.7 us: cost_block(): jnp.einsum('fi,fj->ij', block, others, precision=lax.Precision.HIGHEST)]
    all_gather x4 -> x0, blocking collectives: 88.1 us -> none  [the longest x1 31.6 us: local(): lax.all_gather(src_feat, 'tgt', axis=1, tiled=True)]
    reduce_scatter x1 -> x0, waiting for transfers between devices: 77.8 us -> none  [local(): bary_map = lax.psum_scatter(numer, 'tgt', scatter_dimension=1, tiled=True)]
    all_to_all x0 -> x4, blocking collectives: none -> 55.5 us  [exchange(): return lax.all_to_all(v, axes, 0, 0, tiled=True)]
    pallas_call x0 -> x5, Pallas kernels: none -> 19.6 us  [call(): pl.pallas_call(body, out_shape=[jax.ShapeDtypeStruct(s, f32) for s in out...]
    all_to_all x0 -> x1, waiting for transfers between devices: none -> 15.5 us  [exchange(): return lax.all_to_all(v, axes, 0, 0, tiled=True)]
where the time goes in v1:
time: 97.2 us; the launch traced here: 96.7 us
  blocking collectives  55.5 us (57%)
  Pallas kernels  19.6 us (20%)
  waiting for transfers between devices  15.5 us (16%)
  starting transfers between devices  4.08 us (4%)
  local copies, waits for them, and re-layouts  1.37 us (1%)
    all_to_all x4, blocking collectives, exchange(): return lax.all_to_all(v, axes, 0, 0, tiled=True)  55.5 us
    pallas_call x5, Pallas kernels, call(): pl.pallas_call(body, out_shape=[jax.ShapeDtypeStruct(s, f32) for s in out...  19.6 us
    all_to_all x1, waiting for transfers between devices, exchange(): return lax.all_to_all(v, axes, 0, 0, tiled=True)  15.5 us
    all_to_all x1, starting transfers between devices, exchange(): return lax.all_to_all(v, axes, 0, 0, tiled=True)  4.08 us
  transfers between devices with their start and end apart: 1, of which 1 were waited for; matrix products, arithmetic and copies ran while one was open for 0% of the time, Pallas kernels for 0%

profile of v1, /device:TPU:1, one launch (start us, length us, event | category | flops | bytes accessed | tf_op | source)
XLA Modules:
  0.0 96.7 jit_solution(6773933599305647923)
XLA Ops:
  0.6 0.0 copy-start
  0.6 0.0 copy-start.2
  0.7 0.0 copy-start.3
  0.7 0.0 copy-start.4
  0.7 0.7 copy-done
  1.3 0.0 copy-done.2
  1.3 0.0 copy-done.3
  1.3 0.0 copy-done.4
  1.3 0.0 copy-start.1
  1.3 0.7 copy-done.1
  2.1 10.8 %all_to_all.25.sall = f32[8,17,128]{2,1,0:T(8,128)S(1)} all-to-all(f32[8,17,128]{2,1,0:T(8,128)S(1)} %get-tuple-element.10), channel_id=1, replica_groups=mesh['z'=8,'y'=4,'x'=4,'c'=2] {'y','c'}, dimensions={0} | all-to-all | bytes 139264 | tf_op jit(solution)/shard_map/all_to_all | solution.py:181
  12.8 24.7 %all_to_all.26.tall = f32[32,19,128]{2,1,0:T(8,128)S(1)} all-to-all(f32[32,19,128]{2,1,0:T(8,128)S(1)} %get-tuple-element.9), channel_id=1, replica_groups=mesh['z'=8,'y'=4,'x'=4,'c'=2] {'z','x'}, dimensions={0} | all-to-all | bytes 622592 | tf_op jit(solution)/shard_map/all_to_all | solution.py:181
  37.5 4.3 %shard_map.77 = f32[8,10,128]{2,1,0:T(8,128)S(1)} custom-call(f32[32,19,128]{2,1,0:T(8,128)S(1)} %all_to_all.26.tall, f32[8,17,128]{2,1,0:T(8,128)S(1)} %all_to_all.25.sall), custom_call_target="tpu_custom_call" | custom-call | tf_op jit(solution)/shard_map/pallas_call | solution.py:170
  41.9 9.7 %all_to_all.27.part.first = f32[8,10,128]{2,1,0:T(8,128)S(1)} all-to-all(f32[8,10,128]{2,1,0:T(8,128)S(1)} %shard_map.77), channel_id=1, replica_groups=mesh['z'=8,'y'=4,'x'=4,'c'=2] {'y','c'}, dimensions={0} | all-to-all | bytes 81920 | tf_op jit(solution)/shard_map/all_to_all | solution.py:181
  51.5 5.5 %shard_map.78 = f32[32,32,128]{2,1,0:T(8,128)} custom-call(f32[8,10,128]{2,1,0:T(8,128)S(1)} %all_to_all.27.part.first, f32[32,19,128]{2,1,0:T(8,128)S(1)} %all_to_all.26.tall, f32[8,17,128]{2,1,0:T(8,128)S(1)} %all_to_all.25.sall), custom_call_target="tpu_custom_call" | custom-call | tf_op jit(solution)/shard_map/pallas_call | solution.py:170
  57.1 4.1 %all-to-all-start.3 = ((f32[32,32,128]{2,1,0:T(8,128)}), f32[32,32,128]{2,1,0:T(8,128)S(1)}, u32[]{:S(2)}, u32[]{:S(2)}) async-start(f32[32,32,128]{2,1,0:T(8,128)} %shard_map.78), calls=%async_computation.3 | async-start | bytes 1048576 | tf_op jit(solution)/shard_map/all_to_all | solution.py:181
  61.2 15.5 %all-to-all-done.3.part = f32[32,32,128]{2,1,0:T(8,128)S(1)} async-done(((f32[32,32,128]{2,1,0:T(8,128)}), f32[32,32,128]{2,1,0:T(8,128)S(1)}, u32[]{:S(2)}, u32[]{:S(2)}) %all-to-all-start.3) | async-done | bytes 524320 | tf_op jit(solution)/shard_map/all_to_all | solution.py:181
  76.7 9.0 %shard_map.79 = (f32[8,17,128]{2,1,0:T(8,128)S(1)}, f32[8,128]{1,0:T(8,128)}) custom-call(s32[1]{0:T(128)} %bitcast.xat, f32[32,32,128]{2,1,0:T(8,128)S(1)} %all-to-all-done.3.part, f32[8,10,128]{2,1,0:T(8,128)S(1)} %all_to_all.27.part.first, f32[32,19,128]{2,1,0:T(8,128)S(1)} %all_to_all.26.tall, f32[8,17,128]{2,1,0:T(8,128)S(1)} %all_to_all.25.sall), custom_call_target="tpu_custom_call" | custom-call | tf_op jit(solution)/shard_map/pallas_call | solution.py:170
  85.8 10.3 %all_to_all.28.part = f32[8,17,128]{2,1,0:T(8,128)S(1)} all-to-all(f32[8,17,128]{2,1,0:T(8,128)S(1)} %get-tuple-element.11), channel_id=1, replica_groups=mesh['z'=8,'y'=4,'x'=4,'c'=2] {'y','c'}, dimensions={0} | all-to-all | bytes 139264 | tf_op jit(solution)/shard_map/all_to_all | solution.py:181
  96.1 0.6 shard_map.80
  (1 shorter events, 0.0 us)
Async XLA Ops:
  0.6 0.7 copy-start
  0.6 0.7 copy-start.2
  0.7 0.7 copy-start.3
  0.7 0.7 copy-start.4
  1.3 0.7 copy-start.1
  57.1 19.6 %all-to-all-start.3 = ((f32[32,32,128]{2,1,0:T(8,128)}), f32[32,32,128]{2,1,0:T(8,128)S(1)}, u32[]{:S(2)}, u32[]{:S(2)}) async-start(f32[32,32,128]{2,1,0:T(8,128)} %shard_map.78), calls=%async_computation.3 | async-start | bytes 1048576 | tf_op jit(solution)/shard_map/all_to_all | solution.py:181

commit v2 on v1

v2 whole, which is shorter than its diff:
```python
import functools

import jax
import jax.numpy as jnp
from jax import lax
from jax.experimental import pallas as pl
from jax.experimental.pallas import tpu as pltpu
from jax.sharding import Mesh, PartitionSpec as P

f32 = jnp.float32
bf16 = jnp.bfloat16
LOG2E = 1.4426950408889634
LN2 = 0.6931471805599453
epsilon = 0.5
UNIT = LOG2E / epsilon

T_ORDER = (0, 0, 1, 0, 1, 2)
S_ORDER = (0, 1, 0, 2, 1, 0)
COLS = ("z", "x")
ROWS = ("y", "c")


def split3(v):
    hi = v.astype(bf16)
    rest = v - hi.astype(f32)
    mid = rest.astype(bf16)
    return hi, mid, (rest - mid.astype(f32)).astype(bf16)


def bias_rows(row):
    hi, mid, lo = (jnp.broadcast_to(p.astype(f32), (16, 128)) for p in split3(row))
    r = lax.broadcasted_iota(jnp.int32, (16, 128), 0)
    return jnp.where(r == 0, hi, jnp.where(r == 1, mid, jnp.where(r == 2, lo, 0.0))).astype(bf16)


def put_feats(aug, k, feats, order):
    pieces = split3(feats)
    for at, which in enumerate(order):
        aug[at * 16 : at * 16 + 16, k * 128 : k * 128 + 128] = pieces[which]


def fill_tgt(aug, turned, tall, bias):
    n = tall.shape[0]
    aug[112:128, :] = jnp.ones((16, n * 128), bf16)
    if bias is None:
        aug[96:112, :] = jnp.zeros((16, n * 128), bf16)
    for k in range(n):
        put_feats(aug, k, tall[k, 0:16, :], T_ORDER)
        if bias is not None:
            aug[96:112, k * 128 : k * 128 + 128] = bias_rows(bias(k))
            turned[k * 128 : k * 128 + 128, :] = aug[:, k * 128 : k * 128 + 128].T


def fill_src(aug, turned, sall, bias):
    n = sall.shape[0]
    aug[96:112, :] = jnp.ones((16, n * 128), bf16)
    if bias is None:
        aug[112:128, :] = jnp.zeros((16, n * 128), bf16)
    for k in range(n):
        put_feats(aug, k, sall[k, 0:16, :] * (2.0 * UNIT), S_ORDER)
        if bias is not None:
            aug[112:128, k * 128 : k * 128 + 128] = bias_rows(bias(k))
            turned[k * 128 : k * 128 + 128, :] = aug[:, k * 128 : k * 128 + 128].T


def scores(lhs, rhs):
    return lax.dot(lhs, rhs, preferred_element_type=f32)


def sample_top(lhs, rhs, groups):
    rows = lhs.shape[0] // groups
    some = jnp.concatenate([lhs[g * rows : g * rows + 16, :] for g in range(groups)], 0)
    return jnp.max(scores(some, rhs), 0, keepdims=True)


def full_top(lhs, rhs):
    def step(k, top):
        v = scores(lhs[pl.ds(pl.multiple_of(k * 256, 256), 256), :], rhs)
        return jnp.maximum(top, jnp.max(v, 0, keepdims=True))

    return lax.fori_loop(0, lhs.shape[0] // 256, step, jnp.full((1, rhs.shape[1]), -3e38, f32))


def in_range(sums):
    ok = jnp.ones((1, 256), f32)
    for s in sums:
        ok = jnp.minimum(ok, jnp.where(s < 2.0**100, 1.0, 0.0))
    return jnp.min(ok) > 0.5


def lse_blocks(lhs, aug, groups, put):
    blocks = aug.shape[1] // 256
    tops = [sample_top(lhs, aug[:, c * 256 : c * 256 + 256], groups) for c in range(blocks)]
    sums = []
    for c in range(blocks):
        v = scores(lhs[...], aug[:, c * 256 : c * 256 + 256]).reshape(lhs.shape[0] // 8, 8, 256)
        s = jnp.sum(jnp.sum(jnp.exp2(v - tops[c][None]), 0), 0, keepdims=True)
        put(c, tops[c] + jnp.log2(s))
        sums.append(s)

    @pl.when(jnp.logical_not(in_range(sums)))
    def _():
        @pl.loop(0, blocks)
        def _(c):
            rhs = aug[:, pl.ds(pl.multiple_of(c * 256, 256), 256)]
            top = full_top(lhs, rhs)

            def step(k, s):
                v = scores(lhs[pl.ds(pl.multiple_of(k * 256, 256), 256), :], rhs)
                return s + jnp.sum(jnp.exp2(v - top), 0, keepdims=True)

            s = lax.fori_loop(0, lhs.shape[0] // 256, step, jnp.zeros((1, 256), f32))
            put(c, top + jnp.log2(s))


def lse2(parts):
    top = jnp.max(parts, 0)
    return top + jnp.log2(jnp.sum(jnp.exp2(parts - top[None]), 0))


def total(rows):
    return jnp.sum(jnp.sum(rows, 0, keepdims=True), 1, keepdims=True)


def pack_body(zat, src_feat, tgt_feat, src_mass, tgt_mass, g, tmsg, smsg):
    g_own = g[pl.ds(zat[0], 1), :]
    for k in range(tmsg.shape[0]):
        tmsg[k, 0:16, :] = tgt_feat[...]
        tmsg[k, 16:17, :] = g_own
        tmsg[k, 17:18, :] = tgt_mass[...]
        tmsg[k, 18:19, :] = src_mass[...]
    for k in range(smsg.shape[0]):
        smsg[k, 0:16, :] = src_feat[...]
        smsg[k, 16:17, :] = src_mass[...]


def put_line(out):
    def put(c, line):
        for d in range(out.shape[0]):
            out[d, pl.ds(2 * c, 1), :] = line[:, :128]
            out[d, pl.ds(2 * c + 1, 1), :] = line[:, 128:]

    return put


def first_body(tall, sall, out, taug, tturn, saug):
    def bias(k):
        y = tall[k, 0:16, :]
        return UNIT * (tall[k, 16:17, :] - jnp.sum(y * y, 0, keepdims=True))

    fill_tgt(taug, tturn, tall, bias)
    fill_src(saug, None, sall, None)
    lse_blocks(tturn, saug, 16, put_line(out))
    tmass = jnp.sum(tall[:, 17, :], 0, keepdims=True)
    smass = jnp.sum(tall[:, 18, :], 0, keepdims=True)
    for d in range(out.shape[0]):
        out[d, 8:9, :] = smass
        out[d, 9:10, :] = tmass


def second_body(part, tall, sall, out, taug, saug, sturn):
    lse = lse2(part[:, 0:8, :])

    def bias(k):
        return jnp.log2(sall[k, 16:17, :]) - lse[k : k + 1, :]

    fill_tgt(taug, None, tall, None)
    fill_src(saug, sturn, sall, bias)
    lse_blocks(sturn, taug, 4, put_line(out))


def weigh(lhs, taug_rows, rhs, top):
    w = jnp.exp2(scores(lhs, rhs) - top)
    hi = w.astype(bf16)
    lo = (w - hi.astype(f32)).astype(bf16)
    return scores(taug_rows, hi) + scores(taug_rows, lo)


def third_body(xat, part, first, tall, sall, out, pot, taug, tturn, saug, held):
    held[...] = jnp.log2(tall[:, 17, :]) - lse2(part[...])
    fill_tgt(taug, tturn, tall, lambda k: held[k : k + 1, :])
    fill_src(saug, None, sall, None)
    def put(c, acc, top):
        s = acc[64:65, :]
        feats = (acc[0:16, :] + acc[16:32, :] + acc[48:64, :]) / s
        lse = top + jnp.log2(s)
        for h in range(2):
            out[2 * c + h, 0:16, :] = feats[:, h * 128 : h * 128 + 128]
            out[2 * c + h, 16:17, :] = lse[:, h * 128 : h * 128 + 128]

    def rows_of(at, n):
        return jnp.concatenate([taug[32:96, pl.ds(at, n)], taug[112:128, pl.ds(at, n)]], 0)

    blocks, count = saug.shape[1] // 256, tturn.shape[0]
    tops = [sample_top(tturn, saug[:, c * 256 : c * 256 + 256], 16) for c in range(blocks)]
    sums = []
    for c in range(blocks):
        rhs = saug[:, c * 256 : c * 256 + 256]
        acc = jnp.zeros((80, 256), f32)
        for k in range(count // 1024):
            acc = acc + weigh(tturn[k * 1024 : k * 1024 + 1024, :], rows_of(k * 1024, 1024), rhs, tops[c])
        put(c, acc, tops[c])
        sums.append(acc[64:65, :])

    @pl.when(jnp.logical_not(in_range(sums)))
    def _():
        @pl.loop(0, blocks)
        def _(c):
            rhs = saug[:, pl.ds(pl.multiple_of(c * 256, 256), 256)]
            top = full_top(tturn, rhs)

            def step(k, acc):
                at = pl.multiple_of(k * 256, 256)
                return acc + weigh(tturn[pl.ds(at, 256), :], rows_of(at, 256), rhs, top)

            put(c, lax.fori_loop(0, count // 256, step, jnp.zeros((80, 256), f32)), top)

    shift = jnp.log2(total(first[:, 8, :])) - jnp.log2(total(first[:, 9, :]))
    for z in range(pot.shape[0]):
        at = 4 * z + xat[1]
        y = tall[pl.ds(at, 1), 0:16, :][0]
        pot[z : z + 1, :] = (held[pl.ds(at, 1), :] + shift) / UNIT + jnp.sum(y * y, 0, keepdims=True)


def last_body(part, first, feat, mass, pot, bary):
    lses = part[:, 16, :]
    top = jnp.max(lses, 0, keepdims=True)
    w = jnp.exp2(lses - top)
    s = jnp.sum(w, 0, keepdims=True)
    acc = jnp.zeros((16, 128), f32)
    for k in range(part.shape[0]):
        acc = acc + part[k, 0:16, :] * w[k : k + 1, :]
    bary[...] = acc / s
    shift = jnp.log2(total(first[:, 9, :])) - 2.0 * jnp.log2(total(first[:, 8, :]))
    x = feat[...]
    lse = top + jnp.log2(s)
    pot[...] = (jnp.log2(mass[...]) - lse + shift) / UNIT + jnp.sum(x * x, 0, keepdims=True)


def call(body, outs, args, scratch=(), scalars=0):
    vmem = pl.BlockSpec(memory_space=pltpu.VMEM)
    smem = pl.BlockSpec(memory_space=pltpu.SMEM)
    return pl.pallas_call(
        body,
        out_shape=[jax.ShapeDtypeStruct(s, f32) for s in outs],
        in_specs=[smem] * scalars + [vmem] * (len(args) - scalars),
        out_specs=[vmem] * len(outs),
        scratch_shapes=list(scratch),
        compiler_params=pltpu.CompilerParams(vmem_limit_bytes=48 << 20),
    )(*args)


def exchange(v, axes):
    return lax.all_to_all(v, axes, 0, 0, tiled=True)


def local(src_feat, tgt_feat, src_mass, tgt_mass, g_init):
    at = jnp.stack([lax.axis_index("z"), lax.axis_index("x")])
    smass = src_mass.reshape(1, 128)
    nt, ns = 32, 8
    taug, tturn = pltpu.VMEM((128, nt * 128), bf16), pltpu.VMEM((nt * 128, 128), bf16)
    saug, sturn = pltpu.VMEM((128, ns * 128), bf16), pltpu.VMEM((ns * 128, 128), bf16)
    tmsg, smsg = call(
        pack_body,
        [(nt, 19, 128), (ns, 17, 128)],
        (at, src_feat, tgt_feat, smass, tgt_mass.reshape(1, 128), g_init.reshape(8, 128)),
        scalars=1,
    )
    tall = exchange(tmsg, COLS)
    sall = exchange(smsg, ROWS)
    (msg,) = call(first_body, [(ns, 10, 128)], (tall, sall), [taug, tturn, saug])
    first = exchange(msg, ROWS)
    (msg,) = call(second_body, [(nt, nt, 128)], (first, tall, sall), [taug, saug, sturn])
    second = exchange(msg, COLS)
    msg, tgt_pot = call(
        third_body,
        [(ns, 17, 128), (8, 128)],
        (at, second, first, tall, sall),
        [taug, tturn, saug, pltpu.VMEM((nt, 128), f32)],
        scalars=1,
    )
    third = exchange(msg, ROWS)
    src_pot, bary = call(last_body, [(1, 128), (16, 128)], (third, first, src_feat, smass))
    return src_pot.reshape(128), tgt_pot.reshape(1024), bary


def solution(mesh):
    axes = ("z", "y", "x", "c")
    split = Mesh(mesh.devices.reshape(8, 4, 4, 2), axes)
    src, tgt = ("z", "y", "x", "c"), ("y", "x", "c", "z")
    return jax.shard_map(
        local,
        mesh=split,
        in_specs=(P(None, src), P(None, tgt), P(src), P(tgt), P(("y", "x", "c"))),
        out_specs=(P(src), P(("y", "x", "c")), P(None, src)),
        check_vma=False,
    )
```

time: 97.2 us -> 91.3 us (0.939)
  blocking collectives: 55.5 us -> 74.9 us
  waiting for transfers between devices: 15.5 us -> 0 us
  Pallas kernels: 19.6 us -> 14.7 us
  starting transfers between devices: 4.08 us -> 0 us
    all_to_all x4 -> x5, blocking collectives: 55.5 us -> 74.9 us  [exchange(): return lax.all_to_all(v, axes, 0, 0, tiled=True)]
    all_to_all x1 -> x0, waiting for transfers between devices: 15.5 us -> none  [exchange(): return lax.all_to_all(v, axes, 0, 0, tiled=True)]
    pallas_call x5, Pallas kernels: 19.6 us -> 14.7 us  [call(): pl.pallas_call(body, out_shape=[jax.ShapeDtypeStruct(s, f32) for s in out...]
    all_to_all x1 -> x0, starting transfers between devices: 4.08 us -> none  [exchange(): return lax.all_to_all(v, axes, 0, 0, tiled=True)]
  transfers between devices with their start and end apart: 1 -> 0, of which waited for: 1 -> 0; matrix products, arithmetic and copies ran while one was open for 0% -> 0% of each run, Pallas kernels for 0% -> 0%
where the time goes in v2:
time: 91.3 us; the launch traced here: 91 us
  blocking collectives  74.9 us (82%)
  Pallas kernels  14.7 us (16%)
    all_to_all x5, blocking collectives, exchange(): return lax.all_to_all(v, axes, 0, 0, tiled=True)  74.9 us
    pallas_call x5, Pallas kernels, call(): pl.pallas_call(body, out_shape=[jax.ShapeDtypeStruct(s, f32) for s in out...  14.7 us

profile of v2, /device:TPU:1, one launch (start us, length us, event | category | flops | bytes accessed | tf_op | source)
XLA Modules:
  0.0 91.0 jit_solution(17799713555596226426)
XLA Ops:
  0.6 0.0 copy-start.4
  0.6 0.0 copy-start.2
  0.7 0.0 copy-start.1
  0.7 0.0 copy-start
  0.7 0.1 pad_add_fusion.zat.xat
  0.7 0.0 copy-start.3
  0.8 0.5 copy-done.4
  1.3 0.0 copy-done.2
  1.3 0.0 copy-done.1
  1.4 0.0 copy-done
  1.4 0.0 copy-done.3
  1.4 0.6 shard_map.76
  2.0 10.8 %all_to_all.25.sall = f32[8,17,128]{2,1,0:T(8,128)S(1)} all-to-all(f32[8,17,128]{2,1,0:T(8,128)S(1)} %get-tuple-element.10), channel_id=1, replica_groups=mesh['z'=8,'y'=4,'x'=4,'c'=2] {'y','c'}, dimensions={0} | all-to-all | bytes 139264 | tf_op jit(solution)/shard_map/all_to_all | solution.py:254
  12.8 24.7 %all_to_all.26.tall = f32[32,19,128]{2,1,0:T(8,128)S(1)} all-to-all(f32[32,19,128]{2,1,0:T(8,128)S(1)} %get-tuple-element.9), channel_id=1, replica_groups=mesh['z'=8,'y'=4,'x'=4,'c'=2] {'z','x'}, dimensions={0} | all-to-all | bytes 622592 | tf_op jit(solution)/shard_map/all_to_all | solution.py:254
  37.5 3.0 %shard_map.77 = f32[8,10,128]{2,1,0:T(8,128)S(1)} custom-call(f32[32,19,128]{2,1,0:T(8,128)S(1)} %all_to_all.26.tall, f32[8,17,128]{2,1,0:T(8,128)S(1)} %all_to_all.25.sall), custom_call_target="tpu_custom_call" | custom-call | tf_op jit(solution)/shard_map/pallas_call | solution.py:243
  40.5 9.7 %all_to_all.27.part.first = f32[8,10,128]{2,1,0:T(8,128)S(1)} all-to-all(f32[8,10,128]{2,1,0:T(8,128)S(1)} %shard_map.77), channel_id=1, replica_groups=mesh['z'=8,'y'=4,'x'=4,'c'=2] {'y','c'}, dimensions={0} | all-to-all | bytes 81920 | tf_op jit(solution)/shard_map/all_to_all | solution.py:254
  50.2 3.3 %shard_map.78 = f32[32,32,128]{2,1,0:T(8,128)S(1)} custom-call(f32[8,10,128]{2,1,0:T(8,128)S(1)} %all_to_all.27.part.first, f32[32,19,128]{2,1,0:T(8,128)S(1)} %all_to_all.26.tall, f32[8,17,128]{2,1,0:T(8,128)S(1)} %all_to_all.25.sall), custom_call_target="tpu_custom_call" | custom-call | tf_op jit(solution)/shard_map/pallas_call | solution.py:243
  53.5 19.4 %all_to_all.28.part = f32[32,32,128]{2,1,0:T(8,128)S(1)} all-to-all(f32[32,32,128]{2,1,0:T(8,128)S(1)} %shard_map.78), channel_id=1, replica_groups=mesh['z'=8,'y'=4,'x'=4,'c'=2] {'z','x'}, dimensions={0} | all-to-all | bytes 1048576 | tf_op jit(solution)/shard_map/all_to_all | solution.py:254
  72.9 7.1 %shard_map.79 = (f32[8,17,128]{2,1,0:T(8,128)S(1)}, f32[8,128]{1,0:T(8,128)}) custom-call(s32[2]{0:T(128)S(1)} %pad_add_fusion.zat.xat, f32[32,32,128]{2,1,0:T(8,128)S(1)} %all_to_all.28.part, f32[8,10,128]{2,1,0:T(8,128)S(1)} %all_to_all.27.part.first, f32[32,19,128]{2,1,0:T(8,128)S(1)} %all_to_all.26.tall, f32[8,17,128]{2,1,0:T(8,128)S(1)} %all_to_all.25.sall), custom_call_target="tpu_custom_call" | custom-call | tf_op jit(solution)/shard_map/pallas_call | solution.py:243
  80.0 10.3 %all_to_all.29.part = f32[8,17,128]{2,1,0:T(8,128)S(1)} all-to-all(f32[8,17,128]{2,1,0:T(8,128)S(1)} %get-tuple-element.11), channel_id=1, replica_groups=mesh['z'=8,'y'=4,'x'=4,'c'=2] {'y','c'}, dimensions={0} | all-to-all | bytes 139264 | tf_op jit(solution)/shard_map/all_to_all | solution.py:254
  90.4 0.6 shard_map.80
Async XLA Ops:
  0.6 0.7 copy-start.4
  0.6 0.7 copy-start.2
  0.7 0.7 copy-start.1
  0.7 0.7 copy-start
  0.7 0.7 copy-start.3

commit v3 on v2

--- a/solution.py
+++ b/solution.py
@@ -16,8 +16,8 @@
 
 T_ORDER = (0, 0, 1, 0, 1, 2)
 S_ORDER = (0, 1, 0, 2, 1, 0)
-COLS = ("z", "x")
-ROWS = ("y", "c")
+COLS = ("z", "c")
+ROWS = ("y", "x")
 
 
 def split3(v):
@@ -51,13 +51,21 @@
             turned[k * 128 : k * 128 + 128, :] = aug[:, k * 128 : k * 128 + 128].T
 
 
+def place(k):
+    def pos(to, own):
+        step = (to - own + 4) % 4
+        return jnp.where(step == 0, 0, jnp.where(step == 1, 2, jnp.where(step == 2, 3, 1)))
+
+    return pos(k // 4, lax.axis_index("y")) * 4 + pos(k % 4, lax.axis_index("x"))
+
+
 def fill_src(aug, turned, sall, bias):
     n = sall.shape[0]
     aug[96:112, :] = jnp.ones((16, n * 128), bf16)
     if bias is None:
         aug[112:128, :] = jnp.zeros((16, n * 128), bf16)
     for k in range(n):
-        put_feats(aug, k, sall[k, 0:16, :] * (2.0 * UNIT), S_ORDER)
+        put_feats(aug, k, sall[place(k), 0:16, :] * (2.0 * UNIT), S_ORDER)
         if bias is not None:
             aug[112:128, k * 128 : k * 128 + 128] = bias_rows(bias(k))
             turned[k * 128 : k * 128 + 128, :] = aug[:, k * 128 : k * 128 + 128].T
@@ -88,8 +96,8 @@
     return jnp.min(ok) > 0.5
 
 
-def lse_blocks(lhs, aug, groups, put):
-    blocks = aug.shape[1] // 256
+def lse_blocks(lhs, aug, put):
+    blocks, groups = aug.shape[1] // 256, lhs.shape[0] // 256
     tops = [sample_top(lhs, aug[:, c * 256 : c * 256 + 256], groups) for c in range(blocks)]
     sums = []
     for c in range(blocks):
@@ -122,16 +130,20 @@
     return jnp.sum(jnp.sum(rows, 0, keepdims=True), 1, keepdims=True)
 
 
-def pack_body(zat, src_feat, tgt_feat, src_mass, tgt_mass, g, tmsg, smsg):
-    g_own = g[pl.ds(zat[0], 1), :]
+def pack_body(*refs):
+    ins, tmsg, held, sems = refs[:4], refs[4], refs[5:9], refs[9]
+    copies = [pltpu.make_async_copy(a, b, sems.at[n]) for n, (a, b) in enumerate(zip(ins, held))]
+    for copy in copies:
+        copy.start()
+    for copy in copies:
+        copy.wait()
+    tgt_feat, src_mass, tgt_mass, g = held
+    g_own = g[pl.ds(lax.axis_index("z"), 1), :]
     for k in range(tmsg.shape[0]):
         tmsg[k, 0:16, :] = tgt_feat[...]
         tmsg[k, 16:17, :] = g_own
         tmsg[k, 17:18, :] = tgt_mass[...]
         tmsg[k, 18:19, :] = src_mass[...]
-    for k in range(smsg.shape[0]):
-        smsg[k, 0:16, :] = src_feat[...]
-        smsg[k, 16:17, :] = src_mass[...]
 
 
 def put_line(out):
@@ -143,30 +155,27 @@
     return put
 
 
-def first_body(tall, sall, out, taug, tturn, saug):
+def first_body(tall, sall, mass, out, taug, tturn, saug):
     def bias(k):
         y = tall[k, 0:16, :]
         return UNIT * (tall[k, 16:17, :] - jnp.sum(y * y, 0, keepdims=True))
 
     fill_tgt(taug, tturn, tall, bias)
     fill_src(saug, None, sall, None)
-    lse_blocks(tturn, saug, 16, put_line(out))
-    tmass = jnp.sum(tall[:, 17, :], 0, keepdims=True)
-    smass = jnp.sum(tall[:, 18, :], 0, keepdims=True)
+    lse_blocks(tturn, saug, put_line(out))
     for d in range(out.shape[0]):
-        out[d, 8:9, :] = smass
-        out[d, 9:10, :] = tmass
+        out[d, 16:17, :] = mass[...]
 
 
 def second_body(part, tall, sall, out, taug, saug, sturn):
-    lse = lse2(part[:, 0:8, :])
+    lse = lse2(part[:, 0:16, :])
 
     def bias(k):
-        return jnp.log2(sall[k, 16:17, :]) - lse[k : k + 1, :]
+        return jnp.log2(part[k, 16:17, :]) - lse[k : k + 1, :]
 
     fill_tgt(taug, None, tall, None)
     fill_src(saug, sturn, sall, bias)
-    lse_blocks(sturn, taug, 4, put_line(out))
+    lse_blocks(sturn, taug, put_line(out))
 
 
 def weigh(lhs, taug_rows, rhs, top):
@@ -176,7 +185,7 @@
     return scores(taug_rows, hi) + scores(taug_rows, lo)
 
 
-def third_body(xat, part, first, tall, sall, out, pot, taug, tturn, saug, held):
+def third_body(part, tall, sall, out, pot, taug, tturn, saug, held):
     held[...] = jnp.log2(tall[:, 17, :]) - lse2(part[...])
     fill_tgt(taug, tturn, tall, lambda k: held[k : k + 1, :])
     fill_src(saug, None, sall, None)
@@ -192,7 +201,7 @@
         return jnp.concatenate([taug[32:96, pl.ds(at, n)], taug[112:128, pl.ds(at, n)]], 0)
 
     blocks, count = saug.shape[1] // 256, tturn.shape[0]
-    tops = [sample_top(tturn, saug[:, c * 256 : c * 256 + 256], 16) for c in range(blocks)]
+    tops = [sample_top(tturn, saug[:, c * 256 : c * 256 + 256], count // 256) for c in range(blocks)]
     sums = []
     for c in range(blocks):
         rhs = saug[:, c * 256 : c * 256 + 256]
@@ -215,14 +224,17 @@
 
             put(c, lax.fori_loop(0, count // 256, step, jnp.zeros((80, 256), f32)), top)
 
-    shift = jnp.log2(total(first[:, 8, :])) - jnp.log2(total(first[:, 9, :]))
+    masses = [jnp.sum(tall[:, row, :], 0, keepdims=True) for row in (18, 17)]
+    for d in range(out.shape[0]):
+        out[d, 17:18, :] = masses[0]
+        out[d, 18:19, :] = masses[1]
     for z in range(pot.shape[0]):
-        at = 4 * z + xat[1]
-        y = tall[pl.ds(at, 1), 0:16, :][0]
-        pot[z : z + 1, :] = (held[pl.ds(at, 1), :] + shift) / UNIT + jnp.sum(y * y, 0, keepdims=True)
-
-
-def last_body(part, first, feat, mass, pot, bary):
+        k = 2 * z + lax.axis_index("c")
+        y = tall[pl.ds(k, 1), 0:16, :][0]
+        pot[z : z + 1, :] = held[pl.ds(k, 1), :] / UNIT + jnp.sum(y * y, 0, keepdims=True)
+
+
+def last_body(part, raw, sall, mass, src_pot, tgt_pot, bary):
     lses = part[:, 16, :]
     top = jnp.max(lses, 0, keepdims=True)
     w = jnp.exp2(lses - top)
@@ -231,22 +243,23 @@
     for k in range(part.shape[0]):
         acc = acc + part[k, 0:16, :] * w[k : k + 1, :]
     bary[...] = acc / s
-    shift = jnp.log2(total(first[:, 9, :])) - 2.0 * jnp.log2(total(first[:, 8, :]))
-    x = feat[...]
+    log_a, log_b = jnp.log2(total(part[:, 17, :])), jnp.log2(total(part[:, 18, :]))
+    x = sall[0, 0:16, :]
     lse = top + jnp.log2(s)
-    pot[...] = (jnp.log2(mass[...]) - lse + shift) / UNIT + jnp.sum(x * x, 0, keepdims=True)
-
-
-def call(body, outs, args, scratch=(), scalars=0):
+    src_pot[...] = (jnp.log2(mass[...]) - lse + log_b - 2.0 * log_a) / UNIT + jnp.sum(x * x, 0, keepdims=True)
+    tgt_pot[...] = raw[...] + (log_a - log_b) / UNIT
+
+
+def call(body, outs, args, scratch=(), cost=None, where=pltpu.VMEM, limit=48):
     vmem = pl.BlockSpec(memory_space=pltpu.VMEM)
-    smem = pl.BlockSpec(memory_space=pltpu.SMEM)
     return pl.pallas_call(
         body,
         out_shape=[jax.ShapeDtypeStruct(s, f32) for s in outs],
-        in_specs=[smem] * scalars + [vmem] * (len(args) - scalars),
+        in_specs=[pl.BlockSpec(memory_space=where)] * len(args),
         out_specs=[vmem] * len(outs),
         scratch_shapes=list(scratch),
-        compiler_params=pltpu.CompilerParams(vmem_limit_bytes=48 << 20),
+        cost_estimate=cost,
+        compiler_params=pltpu.CompilerParams(vmem_limit_bytes=limit << 20),
     )(*args)
 
 
@@ -254,33 +267,52 @@
     return lax.all_to_all(v, axes, 0, 0, tiled=True)
 
 
+def join_body(*refs):
+    out, at = refs[-1], 0
+    for ref in refs[:-1]:
+        out[at : at + ref.shape[0]] = ref[...]
+        at += ref.shape[0]
+
+
+def join(parts, flops):
+    shape = (sum(p.shape[0] for p in parts), *parts[0].shape[1:])
+    return call(join_body, [shape], parts, cost=pl.CostEstimate(flops=flops, bytes_accessed=1000, transcendentals=0))[0]
+
+
+def gather_rows(v):
+    for axis in ("x", "y"):
+        moved = [lax.ppermute(v, axis, [(i, (i + by) % 4) for i in range(4)]) for by in (1, 3, 2)]
+        v = join([v, *moved], 10**11) if axis == "x" else jnp.concatenate([v, *moved], 0)
+    return v
+
+
 def local(src_feat, tgt_feat, src_mass, tgt_mass, g_init):
-    at = jnp.stack([lax.axis_index("z"), lax.axis_index("x")])
     smass = src_mass.reshape(1, 128)
-    nt, ns = 32, 8
+    nt, ns = 16, 16
     taug, tturn = pltpu.VMEM((128, nt * 128), bf16), pltpu.VMEM((nt * 128, 128), bf16)
     saug, sturn = pltpu.VMEM((128, ns * 128), bf16), pltpu.VMEM((ns * 128, 128), bf16)
-    tmsg, smsg = call(
+    (tmsg,) = call(
         pack_body,
-        [(nt, 19, 128), (ns, 17, 128)],
-        (at, src_feat, tgt_feat, smass, tgt_mass.reshape(1, 128), g_init.reshape(8, 128)),
-        scalars=1,
+        [(nt, 19, 128)],
+        (tgt_feat, smass, tgt_mass.reshape(1, 128), g_init.reshape(8, 128)),
+        [pltpu.VMEM(s, f32) for s in ((16, 128), (1, 128), (1, 128), (8, 128))] + [pltpu.SemaphoreType.DMA((4,))],
+        where=pltpu.HBM,
+        limit=60,
     )
     tall = exchange(tmsg, COLS)
-    sall = exchange(smsg, ROWS)
-    (msg,) = call(first_body, [(ns, 10, 128)], (tall, sall), [taug, tturn, saug])
+    sall = gather_rows(src_feat.reshape(1, 16, 128))
+    (msg,) = call(first_body, [(ns, ns + 1, 128)], (tall, sall, smass), [taug, tturn, saug])
     first = exchange(msg, ROWS)
     (msg,) = call(second_body, [(nt, nt, 128)], (first, tall, sall), [taug, saug, sturn])
     second = exchange(msg, COLS)
-    msg, tgt_pot = call(
+    msg, raw = call(
         third_body,
-        [(ns, 17, 128), (8, 128)],
-        (at, second, first, tall, sall),
+        [(ns, 19, 128), (8, 128)],
+        (second, tall, sall),
         [taug, tturn, saug, pltpu.VMEM((nt, 128), f32)],
-        scalars=1,
     )
     third = exchange(msg, ROWS)
-    src_pot, bary = call(last_body, [(1, 128), (16, 128)], (third, first, src_feat, smass))
+    src_pot, tgt_pot, bary = call(last_body, [(1, 128), (8, 128), (16, 128)], (third, raw, sall, smass))
     return src_pot.reshape(128), tgt_pot.reshape(1024), bary
 
 

time: 91.3 us -> 78.2 us (0.86)
  blocking collectives: 74.9 us -> 38 us
  starting transfers between devices: 0 us -> 19.6 us
  waiting for transfers between devices: 0 us -> 5.76 us
  Pallas kernels: 14.7 us -> 13.7 us
    all_to_all x5 -> x3, blocking collectives: 74.9 us -> 38 us  [exchange(): return lax.all_to_all(v, axes, 0, 0, tiled=True)]
    all_to_all x0 -> x1, starting transfers between devices: none -> 10 us  [exchange(): return lax.all_to_all(v, axes, 0, 0, tiled=True)]
    ppermute x0 -> x6, starting transfers between devices: none -> 9.62 us  [gather_rows(): lax.ppermute(v, axis, [(i, (i + by) % 4) for i in range(4)])]
    ppermute x0 -> x6, waiting for transfers between devices: none -> 3.59 us  [gather_rows(): lax.ppermute(v, axis, [(i, (i + by) % 4) for i in range(4)])]
    all_to_all x0 -> x1, waiting for transfers between devices: none -> 2.18 us  [exchange(): return lax.all_to_all(v, axes, 0, 0, tiled=True)]
    pallas_call x5 -> x6, Pallas kernels: 14.7 us -> 13.7 us  [call(): pl.pallas_call(body, out_shape=[jax.ShapeDtypeStruct(s, f32) for s in out...]
  transfers between devices with their start and end apart: 0 -> 7, of which waited for: 0 -> 3; matrix products, arithmetic and copies ran while one was open for 0% -> 0% of each run, Pallas kernels for 0% -> 2%
where the time goes in v3:
time: 78.2 us; the launch traced here: 77.8 us
  blocking collectives  38 us (49%)
  starting transfers between devices  19.6 us (25%)
  Pallas kernels  13.7 us (18%)
  waiting for transfers between devices  5.76 us (7%)
    all_to_all x3, blocking collectives, exchange(): return lax.all_to_all(v, axes, 0, 0, tiled=True)  38 us
    pallas_call x6, Pallas kernels, call(): pl.pallas_call(body, out_shape=[jax.ShapeDtypeStruct(s, f32) for s in out...  13.7 us
    all_to_all x1, starting transfers between devices, exchange(): return lax.all_to_all(v, axes, 0, 0, tiled=True)  10 us
    ppermute x6, starting transfers between devices, gather_rows(): lax.ppermute(v, axis, [(i, (i + by) % 4) for i in range(4)])  9.62 us
    ppermute x6, waiting for transfers between devices, gather_rows(): lax.ppermute(v, axis, [(i, (i + by) % 4) for i in range(4)])  3.59 us
    all_to_all x1, waiting for transfers between devices, exchange(): return lax.all_to_all(v, axes, 0, 0, tiled=True)  2.18 us
  transfers between devices with their start and end apart: 7, of which 3 were waited for; matrix products, arithmetic and copies ran while one was open for 0% of the time, Pallas kernels for 2%

profile of v3, /device:TPU:1, one launch (start us, length us, event | category | flops | bytes accessed | tf_op | source)
XLA Modules:
  0.0 77.8 jit_solution(12805156025570524998)
XLA Ops:
  0.6 3.7 %collective-permute-start.2 = (f32[1,16,128]{2,1,0:T(8,128)}, f32[1,16,128]{2,1,0:T(8,128)S(1)}, u32[]{:S(2)}, u32[]{:S(2)}) collective-permute-start(f32[1,16,128]{2,1,0:T(8,128)} %bitcast.9), channel_id=1, source_target_pairs={{0,4},{2,6},{4,0},{6,2},{1,5},{3,7},{5,1},{7,3},{8,12},{10,14},{12... | collective-permute-start | bytes 24584 | tf_op jit(solution)/shard_map/ppermute | solution.py:284
  4.3 0.9 %collective-permute-start.1 = (f32[1,16,128]{2,1,0:T(8,128)}, f32[1,16,128]{2,1,0:T(8,128)S(1)}, u32[]{:S(2)}, u32[]{:S(2)}) collective-permute-start(f32[1,16,128]{2,1,0:T(8,128)} %bitcast.10), channel_id=1, source_target_pairs={{0,6},{2,0},{4,2},{6,4},{1,7},{3,1},{5,3},{7,5},{8,14},{10,8},{12,... | collective-permute-start | bytes 24584 | tf_op jit(solution)/shard_map/ppermute | solution.py:284
  5.2 0.6 collective-permute-start
  5.8 1.5 %shard_map.76 = f32[16,19,128]{2,1,0:T(8,128)} custom-call(f32[16,128]{1,0:T(8,128)} %refs_0_.1, f32[1,128]{1,0:T(1,128)} %bitcast.6, f32[1,128]{1,0:T(1,128)} %bitcast.14, f32[8,128]{1,0:T(8,128)} %bitcast.13), custom_call_target="tpu_custom_call" | custom-call | tf_op jit(solution)/shard_map/pallas_call | solution.py:255
  7.2 0.0 copy-start.1
  7.2 10.0 %all-to-all-start = ((f32[16,19,128]{2,1,0:T(8,128)}), f32[16,19,128]{2,1,0:T(8,128)S(1)}, u32[]{:S(2)}, u32[]{:S(2)}) async-start(f32[16,19,128]{2,1,0:T(8,128)} %shard_map.76), calls=%async_computation | async-start | bytes 393216 | tf_op jit(solution)/shard_map/all_to_all | solution.py:267
  17.3 0.0 collective-permute-done.2.refs_3_
  17.3 0.0 collective-permute-done.1.refs_2_
  17.3 0.0 collective-permute-done.refs_1_
  17.3 0.0 copy-start
  17.3 3.0 %collective-permute-start.5 = (f32[4,16,128]{2,1,0:T(8,128)S(1)}, f32[4,16,128]{2,1,0:T(8,128)S(1)}, u32[]{:S(2)}, u32[]{:S(2)}) collective-permute-start(f32[4,16,128]{2,1,0:T(8,128)S(1)} %shard_map.77), channel_id=1, source_target_pairs={{0,16},{8,24},{16,0},{24,8},{1,17},{9,25},{17,1},{25,9},{2,18},{10... | collective-permute-start | bytes 98312 | tf_op jit(solution)/shard_map/ppermute | solution.py:284
  20.3 0.8 collective-permute-start.4
  21.1 0.7 collective-permute-start.3
  21.8 0.0 collective-permute-done.5
  21.8 1.6 %collective-permute-done.4 = f32[4,16,128]{2,1,0:T(8,128)S(1)} collective-permute-done((f32[4,16,128]{2,1,0:T(8,128)S(1)}, f32[4,16,128]{2,1,0:T(8,128)S(1)}, u32[]{:S(2)}, u32[]{:S(2)}) %collective-permute-start.4) | collective-permute-done | bytes 32800 | tf_op jit(solution)/shard_map/ppermute | solution.py:284
  23.4 2.0 %collective-permute-done.3 = f32[4,16,128]{2,1,0:T(8,128)S(1)} collective-permute-done((f32[4,16,128]{2,1,0:T(8,128)S(1)}, f32[4,16,128]{2,1,0:T(8,128)S(1)}, u32[]{:S(2)}, u32[]{:S(2)}) %collective-permute-start.3) | collective-permute-done | bytes 32800 | tf_op jit(solution)/shard_map/ppermute | solution.py:284
  25.4 2.2 %all-to-all-done.tall = f32[16,19,128]{2,1,0:T(8,128)S(1)} async-done(((f32[16,19,128]{2,1,0:T(8,128)}), f32[16,19,128]{2,1,0:T(8,128)S(1)}, u32[]{:S(2)}, u32[]{:S(2)}) %all-to-all-start) | async-done | bytes 155680 | tf_op jit(solution)/shard_map/all_to_all | solution.py:267
  27.6 2.9 %shard_map.78 = f32[16,17,128]{2,1,0:T(8,128)S(1)} custom-call(f32[16,19,128]{2,1,0:T(8,128)S(1)} %all-to-all-done.tall, f32[16,16,128]{2,1,0:T(8,128)S(1)} %pad_maximum_fusion.sall, f32[1,128]{1,0:T(1,128)S(1)} %bitcast.7), custom_call_target="tpu_custom_call" | custom-call | tf_op jit(solution)/shard_map/pallas_call | solution.py:255
  30.5 13.9 %all_to_all.20.part = f32[16,17,128]{2,1,0:T(8,128)S(1)} all-to-all(f32[16,17,128]{2,1,0:T(8,128)S(1)} %shard_map.78), channel_id=1, replica_groups=mesh['z'=8,'y'=4,'x'=4,'c'=2] {'y','x'}, dimensions={0} | all-to-all | bytes 278528 | tf_op jit(solution)/shard_map/all_to_all | solution.py:267
  44.4 2.9 %shard_map.79 = f32[16,16,128]{2,1,0:T(8,128)S(1)} custom-call(f32[16,17,128]{2,1,0:T(8,128)S(1)} %all_to_all.20.part, f32[16,19,128]{2,1,0:T(8,128)S(1)} %all-to-all-done.tall, f32[16,16,128]{2,1,0:T(8,128)S(1)} %pad_maximum_fusion.sall), custom_call_target="tpu_custom_call" | custom-call | tf_op jit(solution)/shard_map/pallas_call | solution.py:255
  47.3 13.4 %all_to_all.21.part = f32[16,16,128]{2,1,0:T(8,128)S(1)} all-to-all(f32[16,16,128]{2,1,0:T(8,128)S(1)} %shard_map.79), channel_id=1, replica_groups=mesh['z'=8,'y'=4,'x'=4,'c'=2] {'z','c'}, dimensions={0} | all-to-all | bytes 262144 | tf_op jit(solution)/shard_map/all_to_all | solution.py:267
  60.6 5.8 %shard_map.80 = (f32[16,19,128]{2,1,0:T(8,128)S(1)}, f32[8,128]{1,0:T(8,128)S(1)}) custom-call(f32[16,16,128]{2,1,0:T(8,128)S(1)} %all_to_all.21.part, f32[16,19,128]{2,1,0:T(8,128)S(1)} %all-to-all-done.tall, f32[16,16,128]{2,1,0:T(8,128)S(1)} %pad_maximum_fusion.sall), custom_call_target="tpu_custom_call" | custom-call | tf_op jit(solution)/shard_map/pallas_call | solution.py:255
  66.4 10.7 %all_to_all.22.part = f32[16,19,128]{2,1,0:T(8,128)S(1)} all-to-all(f32[16,19,128]{2,1,0:T(8,128)S(1)} %get-tuple-element.8), channel_id=1, replica_groups=mesh['z'=8,'y'=4,'x'=4,'c'=2] {'y','x'}, dimensions={0} | all-to-all | bytes 311296 | tf_op jit(solution)/shard_map/all_to_all | solution.py:267
  77.1 0.7 shard_map.81
  (4 shorter events, 0.0 us)
Async XLA Ops:
  0.6 16.6 %collective-permute-start.2 = (f32[1,16,128]{2,1,0:T(8,128)}, f32[1,16,128]{2,1,0:T(8,128)S(1)}, u32[]{:S(2)}, u32[]{:S(2)}) collective-permute-start(f32[1,16,128]{2,1,0:T(8,128)} %bitcast.9), channel_id=1, source_target_pairs={{0,4},{2,6},{4,0},{6,2},{1,5},{3,7},{5,1},{7,3},{8,12},{10,14},{12... | collective-permute-start | bytes 24584 | tf_op jit(solution)/shard_map/ppermute | solution.py:284
  4.3 13.0 %collective-permute-start.1 = (f32[1,16,128]{2,1,0:T(8,128)}, f32[1,16,128]{2,1,0:T(8,128)S(1)}, u32[]{:S(2)}, u32[]{:S(2)}) collective-permute-start(f32[1,16,128]{2,1,0:T(8,128)} %bitcast.10), channel_id=1, source_target_pairs={{0,6},{2,0},{4,2},{6,4},{1,7},{3,1},{5,3},{7,5},{8,14},{10,8},{12,... | collective-permute-start | bytes 24584 | tf_op jit(solution)/shard_map/ppermute | solution.py:284
  5.2 12.1 %collective-permute-start = (f32[1,16,128]{2,1,0:T(8,128)}, f32[1,16,128]{2,1,0:T(8,128)S(1)}, u32[]{:S(2)}, u32[]{:S(2)}) collective-permute-start(f32[1,16,128]{2,1,0:T(8,128)} %bitcast.11), channel_id=1, source_target_pairs={{0,2},{2,4},{4,6},{6,0},{1,3},{3,5},{5,7},{7,1},{8,10},{10,12},{12... | collective-permute-start | bytes 24584 | tf_op jit(solution)/shard_map/ppermute | solution.py:284
  7.2 10.0 %copy-start.1 = (f32[16,128]{1,0:T(8,128)S(1)}, f32[16,128]{1,0:T(8,128)}, u32[]{:S(2)}) copy-start(f32[16,128]{1,0:T(8,128)} %param.5) | copy-start | bytes 24580
  7.2 20.3 %all-to-all-start = ((f32[16,19,128]{2,1,0:T(8,128)}), f32[16,19,128]{2,1,0:T(8,128)S(1)}, u32[]{:S(2)}, u32[]{:S(2)}) async-start(f32[16,19,128]{2,1,0:T(8,128)} %shard_map.76), calls=%async_computation | async-start | bytes 393216 | tf_op jit(solution)/shard_map/all_to_all | solution.py:267
  17.3 10.3 %copy-start = (f32[128]{0:T(128)S(1)}, f32[128]{0:T(128)}, u32[]{:S(2)}) copy-start(f32[128]{0:T(128)} %param.7) | copy-start | bytes 1540
  17.3 4.5 %collective-permute-start.5 = (f32[4,16,128]{2,1,0:T(8,128)S(1)}, f32[4,16,128]{2,1,0:T(8,128)S(1)}, u32[]{:S(2)}, u32[]{:S(2)}) collective-permute-start(f32[4,16,128]{2,1,0:T(8,128)S(1)} %shard_map.77), channel_id=1, source_target_pairs={{0,16},{8,24},{16,0},{24,8},{1,17},{9,25},{17,1},{25,9},{2,18},{10... | collective-permute-start | bytes 98312 | tf_op jit(solution)/shard_map/ppermute | solution.py:284
  20.3 3.1 %collective-permute-start.4 = (f32[4,16,128]{2,1,0:T(8,128)S(1)}, f32[4,16,128]{2,1,0:T(8,128)S(1)}, u32[]{:S(2)}, u32[]{:S(2)}) collective-permute-start(f32[4,16,128]{2,1,0:T(8,128)S(1)} %shard_map.77), channel_id=1, source_target_pairs={{0,24},{8,0},{16,8},{24,16},{1,25},{9,1},{17,9},{25,17},{2,26},{10... | collective-permute-start | bytes 98312 | tf_op jit(solution)/shard_map/ppermute | solution.py:284
  21.1 4.3 %collective-permute-start.3 = (f32[4,16,128]{2,1,0:T(8,128)S(1)}, f32[4,16,128]{2,1,0:T(8,128)S(1)}, u32[]{:S(2)}, u32[]{:S(2)}) collective-permute-start(f32[4,16,128]{2,1,0:T(8,128)S(1)} %shard_map.77), channel_id=1, source_target_pairs={{0,8},{8,16},{16,24},{24,0},{1,9},{9,17},{17,25},{25,1},{2,10},{10... | collective-permute-start | bytes 98312 | tf_op jit(solution)/shard_map/ppermute | solution.py:284

commit v4 on v3

--- a/solution.py
+++ b/solution.py
@@ -89,36 +89,22 @@
     return lax.fori_loop(0, lhs.shape[0] // 256, step, jnp.full((1, rhs.shape[1]), -3e38, f32))
 
 
-def in_range(sums):
-    ok = jnp.ones((1, 256), f32)
-    for s in sums:
-        ok = jnp.minimum(ok, jnp.where(s < 2.0**100, 1.0, 0.0))
-    return jnp.min(ok) > 0.5
-
-
-def lse_blocks(lhs, aug, put):
-    blocks, groups = aug.shape[1] // 256, lhs.shape[0] // 256
-    tops = [sample_top(lhs, aug[:, c * 256 : c * 256 + 256], groups) for c in range(blocks)]
-    sums = []
-    for c in range(blocks):
-        v = scores(lhs[...], aug[:, c * 256 : c * 256 + 256]).reshape(lhs.shape[0] // 8, 8, 256)
-        s = jnp.sum(jnp.sum(jnp.exp2(v - tops[c][None]), 0), 0, keepdims=True)
-        put(c, tops[c] + jnp.log2(s))
-        sums.append(s)
-
-    @pl.when(jnp.logical_not(in_range(sums)))
-    def _():
-        @pl.loop(0, blocks)
-        def _(c):
-            rhs = aug[:, pl.ds(pl.multiple_of(c * 256, 256), 256)]
-            top = full_top(lhs, rhs)
-
-            def step(k, s):
-                v = scores(lhs[pl.ds(pl.multiple_of(k * 256, 256), 256), :], rhs)
-                return s + jnp.sum(jnp.exp2(v - top), 0, keepdims=True)
-
-            s = lax.fori_loop(0, lhs.shape[0] // 256, step, jnp.zeros((1, 256), f32))
-            put(c, top + jnp.log2(s))
+def exact_lse_blocks(lhs, aug, put, keep=None):
+    @pl.loop(0, aug.shape[1] // 256)
+    def _(c):
+        cols = pl.ds(pl.multiple_of(c * 256, 256), 256)
+        rhs = aug[:, cols]
+        top = full_top(lhs, rhs)
+
+        def step(k, s):
+            rows = pl.ds(pl.multiple_of(k * 256, 256), 256)
+            e = jnp.exp2(scores(lhs[rows, :], rhs) - top)
+            if keep is not None:
+                keep[rows, cols] = e
+            return s + jnp.sum(e, 0, keepdims=True)
+
+        s = lax.fori_loop(0, lhs.shape[0] // 256, step, jnp.zeros((1, 256), f32))
+        put(c, top + jnp.log2(s), top)
 
 
 def lse2(parts):
@@ -130,14 +116,20 @@
     return jnp.sum(jnp.sum(rows, 0, keepdims=True), 1, keepdims=True)
 
 
+def first_bias(tall, k):
+    y = tall[k, 0:16, :]
+    return UNIT * (tall[k, 16:17, :] - jnp.sum(y * y, 0, keepdims=True))
+
+
 def pack_body(*refs):
-    ins, tmsg, held, sems = refs[:4], refs[4], refs[5:9], refs[9]
-    copies = [pltpu.make_async_copy(a, b, sems.at[n]) for n, (a, b) in enumerate(zip(ins, held))]
+    ins, (tmsg, src_feat, src_mass), held, sems = refs[:5], refs[5:8], refs[8:11], refs[11]
+    tgt_feat, tgt_mass, g = held
+    into = (src_feat.at[0], src_mass, tgt_feat, tgt_mass, g)
+    copies = [pltpu.make_async_copy(a, b, sems.at[n]) for n, (a, b) in enumerate(zip(ins, into))]
     for copy in copies:
         copy.start()
     for copy in copies:
         copy.wait()
-    tgt_feat, src_mass, tgt_mass, g = held
     g_own = g[pl.ds(lax.axis_index("z"), 1), :]
     for k in range(tmsg.shape[0]):
         tmsg[k, 0:16, :] = tgt_feat[...]
@@ -147,7 +139,7 @@
 
 
 def put_line(out):
-    def put(c, line):
+    def put(c, line, top=None):
         for d in range(out.shape[0]):
             out[d, pl.ds(2 * c, 1), :] = line[:, :128]
             out[d, pl.ds(2 * c + 1, 1), :] = line[:, 128:]
@@ -155,74 +147,110 @@
     return put
 
 
-def first_body(tall, sall, mass, out, taug, tturn, saug):
-    def bias(k):
-        y = tall[k, 0:16, :]
-        return UNIT * (tall[k, 16:17, :] - jnp.sum(y * y, 0, keepdims=True))
-
-    fill_tgt(taug, tturn, tall, bias)
+def first_body(tall, sall, mass, out, kept, tops, taug, tturn, saug):
+    fill_tgt(taug, tturn, tall, lambda k: first_bias(tall, k))
     fill_src(saug, None, sall, None)
-    lse_blocks(tturn, saug, put_line(out))
+
+    def put(c, line, top):
+        put_line(out)(c, line)
+        tops[pl.ds(2 * c, 1), :] = top[:, :128]
+        tops[pl.ds(2 * c + 1, 1), :] = top[:, 128:]
+
+    blocks, groups = saug.shape[1] // 256, tturn.shape[0] // 256
+    shifts = [sample_top(tturn, saug[:, c * 256 : c * 256 + 256], groups) for c in range(blocks)]
+    ok = jnp.ones((1, 256), f32)
+    for c in range(blocks):
+        e = jnp.exp2(scores(tturn[...], saug[:, c * 256 : c * 256 + 256]) - shifts[c])
+        kept[:, c * 256 : c * 256 + 256] = e
+        s = jnp.sum(jnp.sum(e.reshape(e.shape[0] // 8, 8, 256), 0), 0, keepdims=True)
+        put(c, shifts[c] + jnp.log2(s), shifts[c])
+        ok = jnp.minimum(ok, jnp.where(s < 2.0**40, 1.0, 0.0))
+
+    @pl.when(jnp.min(ok) < 0.5)
+    def _():
+        exact_lse_blocks(tturn, saug, put, kept)
+
     for d in range(out.shape[0]):
         out[d, 16:17, :] = mass[...]
 
 
-def second_body(part, tall, sall, out, taug, saug, sturn):
-    lse = lse2(part[:, 0:16, :])
-
-    def bias(k):
-        return jnp.log2(part[k, 16:17, :]) - lse[k : k + 1, :]
-
-    fill_tgt(taug, None, tall, None)
-    fill_src(saug, sturn, sall, bias)
-    lse_blocks(sturn, taug, put_line(out))
-
-
-def weigh(lhs, taug_rows, rhs, top):
-    w = jnp.exp2(scores(lhs, rhs) - top)
+def second_body(part, kept, tops, tall, sall, out, taug, saug, sturn, held):
+    held[...] = lse2(part[:, 0:16, :])
+    factor = part[:, 16, :] * jnp.exp2(tops[...] - held[...])
+    ok = jnp.ones((1, 128), f32)
+    for k in range(tall.shape[0]):
+        acc = jnp.zeros((128, 128), f32)
+        for r in range(factor.shape[0]):
+            acc = acc + kept[k * 128 : k * 128 + 128, r * 128 : r * 128 + 128] * factor[r : r + 1, :]
+        s = jnp.sum(acc.T, 0, keepdims=True)
+        line = jnp.log2(s) - first_bias(tall, k)
+        for d in range(out.shape[0]):
+            out[d, k : k + 1, :] = line
+        ok = jnp.minimum(ok, jnp.where(s > 2.0**-50, 1.0, 0.0))
+
+    @pl.when(jnp.min(ok) < 0.5)
+    def _():
+        fill_tgt(taug, None, tall, None)
+        fill_src(saug, sturn, sall, lambda k: jnp.log2(part[k, 16:17, :]) - held[k : k + 1, :])
+        exact_lse_blocks(sturn, taug, put_line(out))
+
+
+def weigh(lhs, w):
     hi = w.astype(bf16)
-    lo = (w - hi.astype(f32)).astype(bf16)
-    return scores(taug_rows, hi) + scores(taug_rows, lo)
-
-
-def third_body(part, tall, sall, out, pot, taug, tturn, saug, held):
+    return scores(lhs, hi) + scores(lhs, (w - hi.astype(f32)).astype(bf16))
+
+
+def third_body(part, kept, tops, tall, sall, out, pot, taug, tturn, saug, held, rows):
     held[...] = jnp.log2(tall[:, 17, :]) - lse2(part[...])
-    fill_tgt(taug, tturn, tall, lambda k: held[k : k + 1, :])
-    fill_src(saug, None, sall, None)
+    count, blocks = taug.shape[1], saug.shape[1] // 256
+    bias = jnp.concatenate([first_bias(tall, k) for k in range(tall.shape[0])], 0)
+    ratio = held[...] - bias
+    most = jnp.max(jnp.max(ratio, 0, keepdims=True), 1, keepdims=True)
+    ratio = jnp.exp2(ratio - most)
+
+    def fill_rows(factor):
+        for k in range(tall.shape[0]):
+            f = factor(k)
+            cols = slice(k * 128, k * 128 + 128)
+            rows[0:16, cols], rows[16:32, cols], rows[32:48, cols] = split3(tall[k, 0:16, :] * f)
+            rows[48:64, cols] = bias_rows(f)
+
     def put(c, acc, top):
-        s = acc[64:65, :]
-        feats = (acc[0:16, :] + acc[16:32, :] + acc[48:64, :]) / s
+        s = acc[48:49, :] + acc[49:50, :] + acc[50:51, :]
+        feats = (acc[0:16, :] + acc[16:32, :] + acc[32:48, :]) / s
         lse = top + jnp.log2(s)
         for h in range(2):
             out[2 * c + h, 0:16, :] = feats[:, h * 128 : h * 128 + 128]
             out[2 * c + h, 16:17, :] = lse[:, h * 128 : h * 128 + 128]
-
-    def rows_of(at, n):
-        return jnp.concatenate([taug[32:96, pl.ds(at, n)], taug[112:128, pl.ds(at, n)]], 0)
-
-    blocks, count = saug.shape[1] // 256, tturn.shape[0]
-    tops = [sample_top(tturn, saug[:, c * 256 : c * 256 + 256], count // 256) for c in range(blocks)]
-    sums = []
+        return s
+
+    fill_rows(lambda k: ratio[k : k + 1, :])
+    ok = jnp.ones((1, 256), f32)
     for c in range(blocks):
-        rhs = saug[:, c * 256 : c * 256 + 256]
-        acc = jnp.zeros((80, 256), f32)
+        acc = jnp.zeros((64, 256), f32)
         for k in range(count // 1024):
-            acc = acc + weigh(tturn[k * 1024 : k * 1024 + 1024, :], rows_of(k * 1024, 1024), rhs, tops[c])
-        put(c, acc, tops[c])
-        sums.append(acc[64:65, :])
-
-    @pl.when(jnp.logical_not(in_range(sums)))
+            acc = acc + weigh(rows[:, k * 1024 : k * 1024 + 1024], kept[k * 1024 : k * 1024 + 1024, c * 256 : c * 256 + 256])
+        top = jnp.concatenate([tops[2 * c : 2 * c + 1, :], tops[2 * c + 1 : 2 * c + 2, :]], 1)
+        s = put(c, acc, top + most)
+        ok = jnp.minimum(ok, jnp.where(s > 2.0**-50, 1.0, 0.0))
+
+    @pl.when(jnp.min(ok) < 0.5)
     def _():
+        fill_tgt(taug, tturn, tall, lambda k: held[k : k + 1, :])
+        fill_src(saug, None, sall, None)
+        fill_rows(lambda k: jnp.ones((1, 128), f32))
+
         @pl.loop(0, blocks)
         def _(c):
             rhs = saug[:, pl.ds(pl.multiple_of(c * 256, 256), 256)]
             top = full_top(tturn, rhs)
 
             def step(k, acc):
-                at = pl.multiple_of(k * 256, 256)
-                return acc + weigh(tturn[pl.ds(at, 256), :], rows_of(at, 256), rhs, top)
-
-            put(c, lax.fori_loop(0, count // 256, step, jnp.zeros((80, 256), f32)), top)
+                at = pl.ds(pl.multiple_of(k * 256, 256), 256)
+                return acc + weigh(rows[:, at], jnp.exp2(scores(tturn[at, :], rhs) - top))
+
+            put(c, lax.fori_loop(0, count // 256, step, jnp.zeros((64, 256), f32)), top)
+
 
     masses = [jnp.sum(tall[:, row, :], 0, keepdims=True) for row in (18, 17)]
     for d in range(out.shape[0]):
@@ -279,37 +307,49 @@
     return call(join_body, [shape], parts, cost=pl.CostEstimate(flops=flops, bytes_accessed=1000, transcendentals=0))[0]
 
 
-def gather_rows(v):
+def gather_rows(raw, own):
     for axis in ("x", "y"):
-        moved = [lax.ppermute(v, axis, [(i, (i + by) % 4) for i in range(4)]) for by in (1, 3, 2)]
-        v = join([v, *moved], 10**11) if axis == "x" else jnp.concatenate([v, *moved], 0)
-    return v
+        moved = [lax.ppermute(raw, axis, [(i, (i + by) % 4) for i in range(4)]) for by in (1, 3, 2)]
+        raw = own = join([own, *moved], 10**11) if axis == "x" else jnp.concatenate([own, *moved], 0)
+    return own
 
 
 def local(src_feat, tgt_feat, src_mass, tgt_mass, g_init):
-    smass = src_mass.reshape(1, 128)
     nt, ns = 16, 16
     taug, tturn = pltpu.VMEM((128, nt * 128), bf16), pltpu.VMEM((nt * 128, 128), bf16)
     saug, sturn = pltpu.VMEM((128, ns * 128), bf16), pltpu.VMEM((ns * 128, 128), bf16)
-    (tmsg,) = call(
+    ins = (src_feat, src_mass.reshape(1, 128), tgt_feat, tgt_mass.reshape(1, 128), g_init.reshape(8, 128))
+    tmsg, own, smass = call(
         pack_body,
-        [(nt, 19, 128)],
-        (tgt_feat, smass, tgt_mass.reshape(1, 128), g_init.reshape(8, 128)),
-        [pltpu.VMEM(s, f32) for s in ((16, 128), (1, 128), (1, 128), (8, 128))] + [pltpu.SemaphoreType.DMA((4,))],
+        [(nt, 19, 128), (1, 16, 128), (1, 128)],
+        [pltpu.with_memory_space_constraint(v, pltpu.HBM) for v in ins],
+        [pltpu.VMEM(s, f32) for s in ((16, 128), (1, 128), (8, 128))] + [pltpu.SemaphoreType.DMA((5,))],
         where=pltpu.HBM,
-        limit=60,
     )
     tall = exchange(tmsg, COLS)
-    sall = gather_rows(src_feat.reshape(1, 16, 128))
-    (msg,) = call(first_body, [(ns, ns + 1, 128)], (tall, sall, smass), [taug, tturn, saug])
+    sall = gather_rows(src_feat.reshape(1, 16, 128), own)
+    msg, kept, tops = call(
+        first_body,
+        [(ns, ns + 1, 128), (nt * 128, ns * 128), (ns, 128)],
+        (tall, sall, smass),
+        [taug, tturn, saug],
+        limit=24,
+    )
     first = exchange(msg, ROWS)
-    (msg,) = call(second_body, [(nt, nt, 128)], (first, tall, sall), [taug, saug, sturn])
+    (msg,) = call(
+        second_body,
+        [(nt, nt, 128)],
+        (first, kept, tops, tall, sall),
+        [taug, saug, sturn, pltpu.VMEM((ns, 128), f32)],
+        limit=24,
+    )
     second = exchange(msg, COLS)
     msg, raw = call(
         third_body,
         [(ns, 19, 128), (8, 128)],
-        (second, tall, sall),
-        [taug, tturn, saug, pltpu.VMEM((nt, 128), f32)],
+        (second, kept, tops, tall, sall),
+        [taug, tturn, saug, pltpu.VMEM((nt, 128), f32), pltpu.VMEM((64, nt * 128), bf16)],
+        limit=24,
     )
     third = exchange(msg, ROWS)
     src_pot, tgt_pot, bary = call(last_body, [(1, 128), (8, 128), (16, 128)], (third, raw, sall, smass))

time: 78.2 us -> 74.6 us (0.954)
  Pallas kernels: 13.7 us -> 10.1 us
    pallas_call x6, Pallas kernels: 13.7 us -> 10.1 us  [call(): pl.pallas_call(body, out_shape=[jax.ShapeDtypeStruct(s, f32) for s in out...]
where the time goes in v4:
time: 74.6 us; the launch traced here: 74.2 us
  blocking collectives  38 us (51%)
  starting transfers between devices  19.6 us (26%)
  Pallas kernels  10.1 us (14%)
  waiting for transfers between devices  5.79 us (8%)
    all_to_all x3, blocking collectives, exchange(): return lax.all_to_all(v, axes, 0, 0, tiled=True)  38 us
    pallas_call x6, Pallas kernels, call(): pl.pallas_call(body, out_shape=[jax.ShapeDtypeStruct(s, f32) for s in out...  10.1 us
    all_to_all x1, starting transfers between devices, exchange(): return lax.all_to_all(v, axes, 0, 0, tiled=True)  10 us
    ppermute x6, starting transfers between devices, gather_rows(): lax.ppermute(raw, axis, [(i, (i + by) % 4) for i in range(4)])  9.62 us
    ppermute x6, waiting for transfers between devices, gather_rows(): lax.ppermute(raw, axis, [(i, (i + by) % 4) for i in range(4)])  3.59 us
    all_to_all x1, waiting for transfers between devices, exchange(): return lax.all_to_all(v, axes, 0, 0, tiled=True)  2.2 us
  transfers between devices with their start and end apart: 7, of which 3 were waited for; matrix products, arithmetic and copies ran while one was open for 0% of the time, Pallas kernels for 2%

profile of v4, /device:TPU:1, one launch (start us, length us, event | category | flops | bytes accessed | tf_op | source)
XLA Modules:
  0.0 74.2 jit_solution(11291835235762318659)
XLA Ops:
  0.6 3.7 %collective-permute-start.2 = (f32[1,16,128]{2,1,0:T(8,128)}, f32[1,16,128]{2,1,0:T(8,128)S(1)}, u32[]{:S(2)}, u32[]{:S(2)}) collective-permute-start(f32[1,16,128]{2,1,0:T(8,128)} %bitcast.6), channel_id=1, source_target_pairs={{0,4},{2,6},{4,0},{6,2},{1,5},{3,7},{5,1},{7,3},{8,12},{10,14},{12... | collective-permute-start | bytes 24584 | tf_op jit(solution)/shard_map/ppermute | solution.py:312
  4.3 0.9 %collective-permute-start.1 = (f32[1,16,128]{2,1,0:T(8,128)}, f32[1,16,128]{2,1,0:T(8,128)S(1)}, u32[]{:S(2)}, u32[]{:S(2)}) collective-permute-start(f32[1,16,128]{2,1,0:T(8,128)} %bitcast.7), channel_id=1, source_target_pairs={{0,6},{2,0},{4,2},{6,4},{1,7},{3,1},{5,3},{7,5},{8,14},{10,8},{12,... | collective-permute-start | bytes 24584 | tf_op jit(solution)/shard_map/ppermute | solution.py:312
  5.2 0.6 collective-permute-start
  5.8 1.5 %shard_map.76 = (f32[16,19,128]{2,1,0:T(8,128)}, f32[1,16,128]{2,1,0:T(8,128)S(1)}, f32[1,128]{1,0:T(1,128)S(1)}) custom-call(f32[16,128]{1,0:T(8,128)} %refs_0_.1, f32[1,128]{1,0:T(1,128)} %bitcast.10, f32[16,128]{1,0:T(8,128)} %refs_2_.1, f32[1,128]{1,0:T(1,128)} %bitcast.11, f32[8,128]{1,0:T(8,128)} %bitcast.9), custom_call_target="tpu_custom_call" | custom-call | tf_op jit(solution)/shard_map/pallas_call | solution.py:283
  7.3 10.0 %all-to-all-start = ((f32[16,19,128]{2,1,0:T(8,128)}), f32[16,19,128]{2,1,0:T(8,128)S(1)}, u32[]{:S(2)}, u32[]{:S(2)}) async-start(f32[16,19,128]{2,1,0:T(8,128)} %get-tuple-element.14), calls=%async_computation | async-start | bytes 393216 | tf_op jit(solution)/shard_map/all_to_all | solution.py:295
  17.3 0.0 collective-permute-done.2.refs_3_
  17.3 0.0 collective-permute-done.1.refs_2_
  17.3 0.0 collective-permute-done.refs_1_
  17.3 3.0 %collective-permute-start.5 = (f32[4,16,128]{2,1,0:T(8,128)S(1)}, f32[4,16,128]{2,1,0:T(8,128)S(1)}, u32[]{:S(2)}, u32[]{:S(2)}) collective-permute-start(f32[4,16,128]{2,1,0:T(8,128)S(1)} %shard_map.77), channel_id=1, source_target_pairs={{0,16},{8,24},{16,0},{24,8},{1,17},{9,25},{17,1},{25,9},{2,18},{10... | collective-permute-start | bytes 98312 | tf_op jit(solution)/shard_map/ppermute | solution.py:312
  20.3 0.8 %collective-permute-start.4 = (f32[4,16,128]{2,1,0:T(8,128)S(1)}, f32[4,16,128]{2,1,0:T(8,128)S(1)}, u32[]{:S(2)}, u32[]{:S(2)}) collective-permute-start(f32[4,16,128]{2,1,0:T(8,128)S(1)} %shard_map.77), channel_id=1, source_target_pairs={{0,24},{8,0},{16,8},{24,16},{1,25},{9,1},{17,9},{25,17},{2,26},{10... | collective-permute-start | bytes 98312 | tf_op jit(solution)/shard_map/ppermute | solution.py:312
  21.1 0.7 collective-permute-start.3
  21.8 0.0 collective-permute-done.5
  21.8 1.6 %collective-permute-done.4 = f32[4,16,128]{2,1,0:T(8,128)S(1)} collective-permute-done((f32[4,16,128]{2,1,0:T(8,128)S(1)}, f32[4,16,128]{2,1,0:T(8,128)S(1)}, u32[]{:S(2)}, u32[]{:S(2)}) %collective-permute-start.4) | collective-permute-done | bytes 32800 | tf_op jit(solution)/shard_map/ppermute | solution.py:312
  23.4 2.0 %collective-permute-done.3 = f32[4,16,128]{2,1,0:T(8,128)S(1)} collective-permute-done((f32[4,16,128]{2,1,0:T(8,128)S(1)}, f32[4,16,128]{2,1,0:T(8,128)S(1)}, u32[]{:S(2)}, u32[]{:S(2)}) %collective-permute-start.3) | collective-permute-done | bytes 32800 | tf_op jit(solution)/shard_map/ppermute | solution.py:312
  25.4 2.2 %all-to-all-done.tall = f32[16,19,128]{2,1,0:T(8,128)S(1)} async-done(((f32[16,19,128]{2,1,0:T(8,128)}), f32[16,19,128]{2,1,0:T(8,128)S(1)}, u32[]{:S(2)}, u32[]{:S(2)}) %all-to-all-start) | async-done | bytes 155680 | tf_op jit(solution)/shard_map/all_to_all | solution.py:295
  27.6 2.9 %shard_map.78 = (f32[16,17,128]{2,1,0:T(8,128)S(1)}, f32[2048,2048]{1,0:T(8,128)S(1)}, f32[16,128]{1,0:T(8,128)S(1)}) custom-call(f32[16,19,128]{2,1,0:T(8,128)S(1)} %all-to-all-done.tall, f32[16,16,128]{2,1,0:T(8,128)S(1)} %pad_maximum_fusion.sall, f32[1,128]{1,0:T(1,128)S(1)} %get-tuple-element.16.mass), custom_call_target="tpu_custom_call" | custom-call | tf_op jit(solution)/shard_map/pallas_call | solution.py:283
  30.5 13.9 %all_to_all.20.part = f32[16,17,128]{2,1,0:T(8,128)S(1)} all-to-all(f32[16,17,128]{2,1,0:T(8,128)S(1)} %get-tuple-element.17), channel_id=1, replica_groups=mesh['z'=8,'y'=4,'x'=4,'c'=2] {'y','x'}, dimensions={0} | all-to-all | bytes 278528 | tf_op jit(solution)/shard_map/all_to_all | solution.py:295
  44.4 1.4 %shard_map.79 = f32[16,16,128]{2,1,0:T(8,128)S(1)} custom-call(f32[16,17,128]{2,1,0:T(8,128)S(1)} %all_to_all.20.part, f32[2048,2048]{1,0:T(8,128)S(1)} %get-tuple-element.18.kept, f32[16,128]{1,0:T(8,128)S(1)} %get-tuple-element.19.tops, f32[16,19,128]{2,1,0:T(8,128)S(1)} %all-to-all-done.tall, f32[16,16,128]{2,1,0:T(8,128)S(1)} %pad_maximum_fusion.sall), custom_call_target="tpu_custom_call" | custom-call | tf_op jit(solution)/shard_map/pallas_call | solution.py:283
  45.7 13.4 %all_to_all.21.part = f32[16,16,128]{2,1,0:T(8,128)S(1)} all-to-all(f32[16,16,128]{2,1,0:T(8,128)S(1)} %shard_map.79), channel_id=1, replica_groups=mesh['z'=8,'y'=4,'x'=4,'c'=2] {'z','c'}, dimensions={0} | all-to-all | bytes 262144 | tf_op jit(solution)/shard_map/all_to_all | solution.py:295
  59.1 3.6 %shard_map.80 = (f32[16,19,128]{2,1,0:T(8,128)S(1)}, f32[8,128]{1,0:T(8,128)S(1)}) custom-call(f32[16,16,128]{2,1,0:T(8,128)S(1)} %all_to_all.21.part, f32[2048,2048]{1,0:T(8,128)S(1)} %get-tuple-element.18.kept, f32[16,128]{1,0:T(8,128)S(1)} %get-tuple-element.19.tops, f32[16,19,128]{2,1,0:T(8,128)S(1)} %all-to-all-done.tall, ...), custom_call_target="tpu_custom_call" | custom-call | tf_op jit(solution)/shard_map/pallas_call | solution.py:283
  62.7 10.7 %all_to_all.22.part = f32[16,19,128]{2,1,0:T(8,128)S(1)} all-to-all(f32[16,19,128]{2,1,0:T(8,128)S(1)} %get-tuple-element.20), channel_id=1, replica_groups=mesh['z'=8,'y'=4,'x'=4,'c'=2] {'y','x'}, dimensions={0} | all-to-all | bytes 311296 | tf_op jit(solution)/shard_map/all_to_all | solution.py:295
  73.4 0.7 shard_map.81
  (2 shorter events, 0.0 us)
Async XLA Ops:
  0.6 16.6 %collective-permute-start.2 = (f32[1,16,128]{2,1,0:T(8,128)}, f32[1,16,128]{2,1,0:T(8,128)S(1)}, u32[]{:S(2)}, u32[]{:S(2)}) collective-permute-start(f32[1,16,128]{2,1,0:T(8,128)} %bitcast.6), channel_id=1, source_target_pairs={{0,4},{2,6},{4,0},{6,2},{1,5},{3,7},{5,1},{7,3},{8,12},{10,14},{12... | collective-permute-start | bytes 24584 | tf_op jit(solution)/shard_map/ppermute | solution.py:312
  4.3 13.0 %collective-permute-start.1 = (f32[1,16,128]{2,1,0:T(8,128)}, f32[1,16,128]{2,1,0:T(8,128)S(1)}, u32[]{:S(2)}, u32[]{:S(2)}) collective-permute-start(f32[1,16,128]{2,1,0:T(8,128)} %bitcast.7), channel_id=1, source_target_pairs={{0,6},{2,0},{4,2},{6,4},{1,7},{3,1},{5,3},{7,5},{8,14},{10,8},{12,... | collective-permute-start | bytes 24584 | tf_op jit(solution)/shard_map/ppermute | solution.py:312
  5.2 12.1 %collective-permute-start = (f32[1,16,128]{2,1,0:T(8,128)}, f32[1,16,128]{2,1,0:T(8,128)S(1)}, u32[]{:S(2)}, u32[]{:S(2)}) collective-permute-start(f32[1,16,128]{2,1,0:T(8,128)} %bitcast.8), channel_id=1, source_target_pairs={{0,2},{2,4},{4,6},{6,0},{1,3},{3,5},{5,7},{7,1},{8,10},{10,12},{12... | collective-permute-start | bytes 24584 | tf_op jit(solution)/shard_map/ppermute | solution.py:312
  7.3 20.3 %all-to-all-start = ((f32[16,19,128]{2,1,0:T(8,128)}), f32[16,19,128]{2,1,0:T(8,128)S(1)}, u32[]{:S(2)}, u32[]{:S(2)}) async-start(f32[16,19,128]{2,1,0:T(8,128)} %get-tuple-element.14), calls=%async_computation | async-start | bytes 393216 | tf_op jit(solution)/shard_map/all_to_all | solution.py:295
  17.3 4.5 %collective-permute-start.5 = (f32[4,16,128]{2,1,0:T(8,128)S(1)}, f32[4,16,128]{2,1,0:T(8,128)S(1)}, u32[]{:S(2)}, u32[]{:S(2)}) collective-permute-start(f32[4,16,128]{2,1,0:T(8,128)S(1)} %shard_map.77), channel_id=1, source_target_pairs={{0,16},{8,24},{16,0},{24,8},{1,17},{9,25},{17,1},{25,9},{2,18},{10... | collective-permute-start | bytes 98312 | tf_op jit(solution)/shard_map/ppermute | solution.py:312
  20.3 3.1 %collective-permute-start.4 = (f32[4,16,128]{2,1,0:T(8,128)S(1)}, f32[4,16,128]{2,1,0:T(8,128)S(1)}, u32[]{:S(2)}, u32[]{:S(2)}) collective-permute-start(f32[4,16,128]{2,1,0:T(8,128)S(1)} %shard_map.77), channel_id=1, source_target_pairs={{0,24},{8,0},{16,8},{24,16},{1,25},{9,1},{17,9},{25,17},{2,26},{10... | collective-permute-start | bytes 98312 | tf_op jit(solution)/shard_map/ppermute | solution.py:312
  21.1 4.3 %collective-permute-start.3 = (f32[4,16,128]{2,1,0:T(8,128)S(1)}, f32[4,16,128]{2,1,0:T(8,128)S(1)}, u32[]{:S(2)}, u32[]{:S(2)}) collective-permute-start(f32[4,16,128]{2,1,0:T(8,128)S(1)} %shard_map.77), channel_id=1, source_target_pairs={{0,8},{8,16},{16,24},{24,0},{1,9},{9,17},{17,25},{25,1},{2,10},{10... | collective-permute-start | bytes 98312 | tf_op jit(solution)/shard_map/ppermute | solution.py:312

commit v5 on v4

--- a/solution.py
+++ b/solution.py
@@ -16,7 +16,7 @@
 
 T_ORDER = (0, 0, 1, 0, 1, 2)
 S_ORDER = (0, 1, 0, 2, 1, 0)
-COLS = ("z", "c")
+COLS = ("z",)
 ROWS = ("y", "x")
 
 
@@ -39,13 +39,26 @@
         aug[at * 16 : at * 16 + 16, k * 128 : k * 128 + 128] = pieces[which]
 
 
+class Targets:
+    def __init__(self, mine, other):
+        self.refs, self.count = (mine, other), 2 * mine.shape[0]
+
+    def rows(self, k, first, last):
+        c, z = divmod(k, self.count // 2)
+        mine, other = (ref[z, first:last, :] for ref in self.refs)
+        return jnp.where(lax.axis_index("c") == c, mine, other)
+
+    def line(self, row):
+        return jnp.concatenate([self.rows(k, row, row + 1) for k in range(self.count)], 0)
+
+
 def fill_tgt(aug, turned, tall, bias):
-    n = tall.shape[0]
+    n = tall.count
     aug[112:128, :] = jnp.ones((16, n * 128), bf16)
     if bias is None:
         aug[96:112, :] = jnp.zeros((16, n * 128), bf16)
     for k in range(n):
-        put_feats(aug, k, tall[k, 0:16, :], T_ORDER)
+        put_feats(aug, k, tall.rows(k, 0, 16), T_ORDER)
         if bias is not None:
             aug[96:112, k * 128 : k * 128 + 128] = bias_rows(bias(k))
             turned[k * 128 : k * 128 + 128, :] = aug[:, k * 128 : k * 128 + 128].T
@@ -117,8 +130,8 @@
 
 
 def first_bias(tall, k):
-    y = tall[k, 0:16, :]
-    return UNIT * (tall[k, 16:17, :] - jnp.sum(y * y, 0, keepdims=True))
+    y = tall.rows(k, 0, 16)
+    return UNIT * (tall.rows(k, 16, 17) - jnp.sum(y * y, 0, keepdims=True))
 
 
 def pack_body(*refs):
@@ -147,7 +160,8 @@
     return put
 
 
-def first_body(tall, sall, mass, out, kept, tops, taug, tturn, saug):
+def first_body(mine, other, sall, mass, out, kept, tops, taug, tturn, saug):
+    tall = Targets(mine, other)
     fill_tgt(taug, tturn, tall, lambda k: first_bias(tall, k))
     fill_src(saug, None, sall, None)
 
@@ -174,18 +188,17 @@
         out[d, 16:17, :] = mass[...]
 
 
-def second_body(part, kept, tops, tall, sall, out, taug, saug, sturn, held):
+def second_body(part, kept, tops, mine, other, sall, out, taug, saug, sturn, held):
+    tall = Targets(mine, other)
     held[...] = lse2(part[:, 0:16, :])
     factor = part[:, 16, :] * jnp.exp2(tops[...] - held[...])
     ok = jnp.ones((1, 128), f32)
-    for k in range(tall.shape[0]):
+    for k in range(tall.count):
         acc = jnp.zeros((128, 128), f32)
         for r in range(factor.shape[0]):
             acc = acc + kept[k * 128 : k * 128 + 128, r * 128 : r * 128 + 128] * factor[r : r + 1, :]
         s = jnp.sum(acc.T, 0, keepdims=True)
-        line = jnp.log2(s) - first_bias(tall, k)
-        for d in range(out.shape[0]):
-            out[d, k : k + 1, :] = line
+        out[0, k : k + 1, :] = jnp.log2(s) - first_bias(tall, k)
         ok = jnp.minimum(ok, jnp.where(s > 2.0**-50, 1.0, 0.0))
 
     @pl.when(jnp.min(ok) < 0.5)
@@ -195,24 +208,31 @@
         exact_lse_blocks(sturn, taug, put_line(out))
 
 
+def pair_body(mine, other, out):
+    both = lse2(jnp.concatenate([mine[...], other[...]], 0))
+    for d in range(out.shape[0]):
+        out[d] = both
+
+
 def weigh(lhs, w):
     hi = w.astype(bf16)
     return scores(lhs, hi) + scores(lhs, (w - hi.astype(f32)).astype(bf16))
 
 
-def third_body(part, kept, tops, tall, sall, out, pot, taug, tturn, saug, held, rows):
-    held[...] = jnp.log2(tall[:, 17, :]) - lse2(part[...])
+def third_body(part, kept, tops, mine, other, sall, out, pot, taug, tturn, saug, held, rows):
+    tall = Targets(mine, other)
+    held[...] = jnp.log2(tall.line(17)) - lse2(part[...])
     count, blocks = taug.shape[1], saug.shape[1] // 256
-    bias = jnp.concatenate([first_bias(tall, k) for k in range(tall.shape[0])], 0)
+    bias = jnp.concatenate([first_bias(tall, k) for k in range(tall.count)], 0)
     ratio = held[...] - bias
     most = jnp.max(jnp.max(ratio, 0, keepdims=True), 1, keepdims=True)
     ratio = jnp.exp2(ratio - most)
 
     def fill_rows(factor):
-        for k in range(tall.shape[0]):
+        for k in range(tall.count):
             f = factor(k)
             cols = slice(k * 128, k * 128 + 128)
-            rows[0:16, cols], rows[16:32, cols], rows[32:48, cols] = split3(tall[k, 0:16, :] * f)
+            rows[0:16, cols], rows[16:32, cols], rows[32:48, cols] = split3(tall.rows(k, 0, 16) * f)
             rows[48:64, cols] = bias_rows(f)
 
     def put(c, acc, top):
@@ -252,14 +272,13 @@
             put(c, lax.fori_loop(0, count // 256, step, jnp.zeros((64, 256), f32)), top)
 
 
-    masses = [jnp.sum(tall[:, row, :], 0, keepdims=True) for row in (18, 17)]
+    masses = [jnp.sum(tall.line(row), 0, keepdims=True) for row in (18, 17)]
     for d in range(out.shape[0]):
         out[d, 17:18, :] = masses[0]
         out[d, 18:19, :] = masses[1]
     for z in range(pot.shape[0]):
-        k = 2 * z + lax.axis_index("c")
-        y = tall[pl.ds(k, 1), 0:16, :][0]
-        pot[z : z + 1, :] = held[pl.ds(k, 1), :] / UNIT + jnp.sum(y * y, 0, keepdims=True)
+        y = mine[z, 0:16, :]
+        pot[z : z + 1, :] = held[pl.ds(lax.axis_index("c") * 8 + z, 1), :] / UNIT + jnp.sum(y * y, 0, keepdims=True)
 
 
 def last_body(part, raw, sall, mass, src_pot, tgt_pot, bary):
@@ -278,7 +297,7 @@
     tgt_pot[...] = raw[...] + (log_a - log_b) / UNIT
 
 
-def call(body, outs, args, scratch=(), cost=None, where=pltpu.VMEM, limit=48):
+def call(body, outs, args, scratch=(), cost=None, where=pltpu.VMEM, limit=8):
     vmem = pl.BlockSpec(memory_space=pltpu.VMEM)
     return pl.pallas_call(
         body,
@@ -321,33 +340,35 @@
     ins = (src_feat, src_mass.reshape(1, 128), tgt_feat, tgt_mass.reshape(1, 128), g_init.reshape(8, 128))
     tmsg, own, smass = call(
         pack_body,
-        [(nt, 19, 128), (1, 16, 128), (1, 128)],
+        [(8, 19, 128), (1, 16, 128), (1, 128)],
         [pltpu.with_memory_space_constraint(v, pltpu.HBM) for v in ins],
         [pltpu.VMEM(s, f32) for s in ((16, 128), (1, 128), (8, 128))] + [pltpu.SemaphoreType.DMA((5,))],
         where=pltpu.HBM,
     )
-    tall = exchange(tmsg, COLS)
+    mine = exchange(tmsg, COLS)
+    other = lax.ppermute(mine, "c", [(0, 1), (1, 0)])
     sall = gather_rows(src_feat.reshape(1, 16, 128), own)
     msg, kept, tops = call(
         first_body,
         [(ns, ns + 1, 128), (nt * 128, ns * 128), (ns, 128)],
-        (tall, sall, smass),
+        (mine, other, sall, smass),
         [taug, tturn, saug],
         limit=24,
     )
     first = exchange(msg, ROWS)
     (msg,) = call(
         second_body,
-        [(nt, nt, 128)],
-        (first, kept, tops, tall, sall),
+        [(1, nt, 128)],
+        (first, kept, tops, mine, other, sall),
         [taug, saug, sturn, pltpu.VMEM((ns, 128), f32)],
         limit=24,
     )
+    (msg,) = call(pair_body, [(8, nt, 128)], (msg, lax.ppermute(msg, "c", [(0, 1), (1, 0)])))
     second = exchange(msg, COLS)
     msg, raw = call(
         third_body,
         [(ns, 19, 128), (8, 128)],
-        (second, kept, tops, tall, sall),
+        (second, kept, tops, mine, other, sall),
         [taug, tturn, saug, pltpu.VMEM((nt, 128), f32), pltpu.VMEM((64, nt * 128), bf16)],
         limit=24,
     )

time: 74.6 us -> 73.1 us (0.980)
  blocking collectives: 38 us -> 33.8 us
  starting transfers between devices: 19.6 us -> 22.5 us
  waiting for transfers between devices: 5.79 us -> 4.89 us
    ppermute x0 -> x2, starting transfers between devices: none -> 4.75 us  [the longest x1 2.88 us: local(): other = lax.ppermute(mine, 'c', [(0, 1), (1, 0)])]
    all_to_all x3, blocking collectives: 38 us -> 33.8 us  [exchange(): return lax.all_to_all(v, axes, 0, 0, tiled=True)]
    ppermute x6, waiting for transfers between devices: 3.59 us -> 0.02 us  [gather_rows(): lax.ppermute(raw, axis, [(i, (i + by) % 4) for i in range(4)])]
    all_to_all x1, starting transfers between devices: 10 us -> 8.2 us  [exchange(): return lax.all_to_all(v, axes, 0, 0, tiled=True)]
    ppermute x0 -> x2, waiting for transfers between devices: none -> 1.74 us  [the longest x1 0.91 us: local(): other = lax.ppermute(mine, 'c', [(0, 1), (1, 0)])]
    all_to_all x1, waiting for transfers between devices: 2.2 us -> 3.13 us  [exchange(): return lax.all_to_all(v, axes, 0, 0, tiled=True)]
    pallas_call x6 -> x7, Pallas kernels: 10.1 us -> 10.1 us  [call(): pl.pallas_call(body, out_shape=[jax.ShapeDtypeStruct(s, f32) for s in out...]
  transfers between devices with their start and end apart: 7 -> 9, of which waited for: 3 -> 3; matrix products, arithmetic and copies ran while one was open for 0% -> 0% of each run, Pallas kernels for 2% -> 2%
where the time goes in v5:
time: 73.1 us; the launch traced here: 72 us
  blocking collectives  33.8 us (46%)
  starting transfers between devices  22.5 us (31%)
  Pallas kernels  10.1 us (14%)
  waiting for transfers between devices  4.89 us (7%)
    all_to_all x3, blocking collectives, exchange(): return lax.all_to_all(v, axes, 0, 0, tiled=True)  33.8 us
    pallas_call x7, Pallas kernels, call(): pl.pallas_call(body, out_shape=[jax.ShapeDtypeStruct(s, f32) for s in out...  10.1 us
    ppermute x6, starting transfers between devices, gather_rows(): lax.ppermute(raw, axis, [(i, (i + by) % 4) for i in range(4)])  9.59 us
    all_to_all x1, starting transfers between devices, exchange(): return lax.all_to_all(v, axes, 0, 0, tiled=True)  8.2 us
    all_to_all x1, waiting for transfers between devices, exchange(): return lax.all_to_all(v, axes, 0, 0, tiled=True)  3.13 us
    ppermute x1, starting transfers between devices, local(): other = lax.ppermute(mine, 'c', [(0, 1), (1, 0)])  2.88 us
    ppermute x1, starting transfers between devices, local(): lax.ppermute(msg, 'c', [(0, 1), (1, 0)])  1.87 us
  transfers between devices with their start and end apart: 9, of which 3 were waited for; matrix products, arithmetic and copies ran while one was open for 0% of the time, Pallas kernels for 2%

profile of v5, /device:TPU:1, one launch (start us, length us, event | category | flops | bytes accessed | tf_op | source)
XLA Modules:
  0.0 72.0 jit_solution(17002819552342973161)
XLA Ops:
  0.6 3.7 %collective-permute-start.3 = (f32[1,16,128]{2,1,0:T(8,128)}, f32[1,16,128]{2,1,0:T(8,128)S(1)}, u32[]{:S(2)}, u32[]{:S(2)}) collective-permute-start(f32[1,16,128]{2,1,0:T(8,128)} %bitcast.6), channel_id=1, source_target_pairs={{0,4},{2,6},{4,0},{6,2},{1,5},{3,7},{5,1},{7,3},{8,12},{10,14},{12... | collective-permute-start | bytes 24584 | tf_op jit(solution)/shard_map/ppermute | solution.py:331
  4.3 0.9 %collective-permute-start.2 = (f32[1,16,128]{2,1,0:T(8,128)}, f32[1,16,128]{2,1,0:T(8,128)S(1)}, u32[]{:S(2)}, u32[]{:S(2)}) collective-permute-start(f32[1,16,128]{2,1,0:T(8,128)} %bitcast.7), channel_id=1, source_target_pairs={{0,6},{2,0},{4,2},{6,4},{1,7},{3,1},{5,3},{7,5},{8,14},{10,8},{12,... | collective-permute-start | bytes 24584 | tf_op jit(solution)/shard_map/ppermute | solution.py:331
  5.2 0.6 collective-permute-start.1
  5.8 1.4 %shard_map.76 = (f32[8,19,128]{2,1,0:T(8,128)}, f32[1,16,128]{2,1,0:T(8,128)S(1)}, f32[1,128]{1,0:T(1,128)S(1)}) custom-call(f32[16,128]{1,0:T(8,128)} %refs_0_.1, f32[1,128]{1,0:T(1,128)} %bitcast.10, f32[16,128]{1,0:T(8,128)} %refs_2_.1, f32[1,128]{1,0:T(1,128)} %bitcast.11, f32[8,128]{1,0:T(8,128)} %bitcast.9), custom_call_target="tpu_custom_call" | custom-call | tf_op jit(solution)/shard_map/pallas_call | solution.py:302
  7.2 8.2 %all-to-all-start = ((f32[8,19,128]{2,1,0:T(8,128)}), f32[8,19,128]{2,1,0:T(8,128)S(1)}, u32[]{:S(2)}, u32[]{:S(2)}) async-start(f32[8,19,128]{2,1,0:T(8,128)} %get-tuple-element.14), calls=%async_computation | async-start | bytes 196608 | tf_op jit(solution)/shard_map/all_to_all | solution.py:314
  15.4 0.0 collective-permute-done.3.refs_3_
  15.4 0.0 collective-permute-done.1.refs_1_
  15.4 3.0 %collective-permute-start.6 = (f32[4,16,128]{2,1,0:T(8,128)S(1)}, f32[4,16,128]{2,1,0:T(8,128)S(1)}, u32[]{:S(2)}, u32[]{:S(2)}) collective-permute-start(f32[4,16,128]{2,1,0:T(8,128)S(1)} %shard_map.77), channel_id=1, source_target_pairs={{0,16},{8,24},{16,0},{24,8},{1,17},{9,25},{17,1},{25,9},{2,18},{10... | collective-permute-start | bytes 98312 | tf_op jit(solution)/shard_map/ppermute | solution.py:331
  18.4 0.8 %collective-permute-start.5 = (f32[4,16,128]{2,1,0:T(8,128)S(1)}, f32[4,16,128]{2,1,0:T(8,128)S(1)}, u32[]{:S(2)}, u32[]{:S(2)}) collective-permute-start(f32[4,16,128]{2,1,0:T(8,128)S(1)} %shard_map.77), channel_id=1, source_target_pairs={{0,24},{8,0},{16,8},{24,16},{1,25},{9,1},{17,9},{25,17},{2,26},{10... | collective-permute-start | bytes 98312 | tf_op jit(solution)/shard_map/ppermute | solution.py:331
  19.2 0.7 collective-permute-start.4
  19.9 3.1 %all-to-all-done.mine = f32[8,19,128]{2,1,0:T(8,128)S(1)} async-done(((f32[8,19,128]{2,1,0:T(8,128)}), f32[8,19,128]{2,1,0:T(8,128)S(1)}, u32[]{:S(2)}, u32[]{:S(2)}) %all-to-all-start) | async-done | bytes 77856 | tf_op jit(solution)/shard_map/all_to_all | solution.py:314
  23.0 2.9 %collective-permute-start = (f32[8,19,128]{2,1,0:T(8,128)S(1)}, f32[8,19,128]{2,1,0:T(8,128)S(1)}, u32[]{:S(2)}, u32[]{:S(2)}) collective-permute-start(f32[8,19,128]{2,1,0:T(8,128)S(1)} %all-to-all-done.mine), channel_id=1, source_target_pairs={{0,1},{1,0},{2,3},{3,2},{4,5},{5,4},{6,7},{7,6},{8,9},{9,8},{10,11... | collective-permute-start | bytes 233480 | tf_op jit(solution)/shard_map/ppermute | solution.py:349
  25.9 0.0 collective-permute-done.6
  25.9 0.0 collective-permute-done.5
  25.9 0.9 %collective-permute-done.other = f32[8,19,128]{2,1,0:T(8,128)S(1)} collective-permute-done((f32[8,19,128]{2,1,0:T(8,128)S(1)}, f32[8,19,128]{2,1,0:T(8,128)S(1)}, u32[]{:S(2)}, u32[]{:S(2)}) %collective-permute-start) | collective-permute-done | bytes 77856 | tf_op jit(solution)/shard_map/ppermute | solution.py:349
  26.9 2.9 %shard_map.78 = (f32[16,17,128]{2,1,0:T(8,128)S(1)}, f32[2048,2048]{1,0:T(8,128)S(1)}, f32[16,128]{1,0:T(8,128)S(1)}) custom-call(f32[8,19,128]{2,1,0:T(8,128)S(1)} %all-to-all-done.mine, f32[8,19,128]{2,1,0:T(8,128)S(1)} %collective-permute-done.other, f32[16,16,128]{2,1,0:T(8,128)S(1)} %pad_maximum_fusion.sall, f32[1,128]{1,0:T(1,128)S(1)} %get-tuple-element.16.mass), custom_call_target="tpu_custom_call" | custom-call | tf_op jit(solution)/shard_map/pallas_call | solution.py:302
  29.8 13.1 %all_to_all.20.part = f32[16,17,128]{2,1,0:T(8,128)S(1)} all-to-all(f32[16,17,128]{2,1,0:T(8,128)S(1)} %get-tuple-element.17), channel_id=1, replica_groups=mesh['z'=8,'y'=4,'x'=4,'c'=2] {'y','x'}, dimensions={0} | all-to-all | bytes 278528 | tf_op jit(solution)/shard_map/all_to_all | solution.py:314
  42.8 1.4 %shard_map.79.mine = f32[1,16,128]{2,1,0:T(8,128)S(1)} custom-call(f32[16,17,128]{2,1,0:T(8,128)S(1)} %all_to_all.20.part, f32[2048,2048]{1,0:T(8,128)S(1)} %get-tuple-element.18.kept, f32[16,128]{1,0:T(8,128)S(1)} %get-tuple-element.19.tops, f32[8,19,128]{2,1,0:T(8,128)S(1)} %all-to-all-done.mine, f32[8,19,128]{2,1,0:T(8,128)S(1)} %collective-permute-done.other, ...), custom_call_target="tpu_custom_call" | custom-call | tf_op jit(solution)/shard_map/pallas_call | solution.py:302
  44.2 1.9 %collective-permute-start.7 = (f32[1,16,128]{2,1,0:T(8,128)S(1)}, f32[1,16,128]{2,1,0:T(8,128)S(1)}, u32[]{:S(2)}, u32[]{:S(2)}) collective-permute-start(f32[1,16,128]{2,1,0:T(8,128)S(1)} %shard_map.79.mine), channel_id=1, source_target_pairs={{0,1},{1,0},{2,3},{3,2},{4,5},{5,4},{6,7},{7,6},{8,9},{9,8},{10,11... | collective-permute-start | bytes 24584 | tf_op jit(solution)/shard_map/ppermute | solution.py:366
  46.1 0.8 %collective-permute-done.7.other = f32[1,16,128]{2,1,0:T(8,128)S(1)} collective-permute-done((f32[1,16,128]{2,1,0:T(8,128)S(1)}, f32[1,16,128]{2,1,0:T(8,128)S(1)}, u32[]{:S(2)}, u32[]{:S(2)}) %collective-permute-start.7) | collective-permute-done | bytes 8224 | tf_op jit(solution)/shard_map/ppermute | solution.py:366
  46.9 10.8 %all_to_all.21.part = f32[8,16,128]{2,1,0:T(8,128)S(1)} all-to-all(f32[8,16,128]{2,1,0:T(8,128)S(1)} %shard_map.80), channel_id=1, replica_groups=mesh['z'=8,'y'=4,'x'=4,'c'=2] {'z'}, dimensions={0} | all-to-all | bytes 131072 | tf_op jit(solution)/shard_map/all_to_all | solution.py:314
  57.7 3.7 %shard_map.81 = (f32[16,19,128]{2,1,0:T(8,128)S(1)}, f32[8,128]{1,0:T(8,128)S(1)}) custom-call(f32[8,16,128]{2,1,0:T(8,128)S(1)} %all_to_all.21.part, f32[2048,2048]{1,0:T(8,128)S(1)} %get-tuple-element.18.kept, f32[16,128]{1,0:T(8,128)S(1)} %get-tuple-element.19.tops, f32[8,19,128]{2,1,0:T(8,128)S(1)} %all-to-all-done.mine, ...), custom_call_target="tpu_custom_call" | custom-call | tf_op jit(solution)/shard_map/pallas_call | solution.py:302
  61.4 9.9 %all_to_all.22.part = f32[16,19,128]{2,1,0:T(8,128)S(1)} all-to-all(f32[16,19,128]{2,1,0:T(8,128)S(1)} %get-tuple-element.20), channel_id=1, replica_groups=mesh['z'=8,'y'=4,'x'=4,'c'=2] {'y','x'}, dimensions={0} | all-to-all | bytes 311296 | tf_op jit(solution)/shard_map/all_to_all | solution.py:314
  71.3 0.7 shard_map.82
  (5 shorter events, 0.0 us)
Async XLA Ops:
  0.6 14.8 %collective-permute-start.3 = (f32[1,16,128]{2,1,0:T(8,128)}, f32[1,16,128]{2,1,0:T(8,128)S(1)}, u32[]{:S(2)}, u32[]{:S(2)}) collective-permute-start(f32[1,16,128]{2,1,0:T(8,128)} %bitcast.6), channel_id=1, source_target_pairs={{0,4},{2,6},{4,0},{6,2},{1,5},{3,7},{5,1},{7,3},{8,12},{10,14},{12... | collective-permute-start | bytes 24584 | tf_op jit(solution)/shard_map/ppermute | solution.py:331
  4.3 11.1 %collective-permute-start.2 = (f32[1,16,128]{2,1,0:T(8,128)}, f32[1,16,128]{2,1,0:T(8,128)S(1)}, u32[]{:S(2)}, u32[]{:S(2)}) collective-permute-start(f32[1,16,128]{2,1,0:T(8,128)} %bitcast.7), channel_id=1, source_target_pairs={{0,6},{2,0},{4,2},{6,4},{1,7},{3,1},{5,3},{7,5},{8,14},{10,8},{12,... | collective-permute-start | bytes 24584 | tf_op jit(solution)/shard_map/ppermute | solution.py:331
  5.2 10.3 %collective-permute-start.1 = (f32[1,16,128]{2,1,0:T(8,128)}, f32[1,16,128]{2,1,0:T(8,128)S(1)}, u32[]{:S(2)}, u32[]{:S(2)}) collective-permute-start(f32[1,16,128]{2,1,0:T(8,128)} %bitcast.8), channel_id=1, source_target_pairs={{0,2},{2,4},{4,6},{6,0},{1,3},{3,5},{5,7},{7,1},{8,10},{10,12},{12... | collective-permute-start | bytes 24584 | tf_op jit(solution)/shard_map/ppermute | solution.py:331
  7.2 15.8 %all-to-all-start = ((f32[8,19,128]{2,1,0:T(8,128)}), f32[8,19,128]{2,1,0:T(8,128)S(1)}, u32[]{:S(2)}, u32[]{:S(2)}) async-start(f32[8,19,128]{2,1,0:T(8,128)} %get-tuple-element.14), calls=%async_computation | async-start | bytes 196608 | tf_op jit(solution)/shard_map/all_to_all | solution.py:314
  15.4 10.5 %collective-permute-start.6 = (f32[4,16,128]{2,1,0:T(8,128)S(1)}, f32[4,16,128]{2,1,0:T(8,128)S(1)}, u32[]{:S(2)}, u32[]{:S(2)}) collective-permute-start(f32[4,16,128]{2,1,0:T(8,128)S(1)} %shard_map.77), channel_id=1, source_target_pairs={{0,16},{8,24},{16,0},{24,8},{1,17},{9,25},{17,1},{25,9},{2,18},{10... | collective-permute-start | bytes 98312 | tf_op jit(solution)/shard_map/ppermute | solution.py:331
  18.4 7.5 %collective-permute-start.5 = (f32[4,16,128]{2,1,0:T(8,128)S(1)}, f32[4,16,128]{2,1,0:T(8,128)S(1)}, u32[]{:S(2)}, u32[]{:S(2)}) collective-permute-start(f32[4,16,128]{2,1,0:T(8,128)S(1)} %shard_map.77), channel_id=1, source_target_pairs={{0,24},{8,0},{16,8},{24,16},{1,25},{9,1},{17,9},{25,17},{2,26},{10... | collective-permute-start | bytes 98312 | tf_op jit(solution)/shard_map/ppermute | solution.py:331
  19.2 6.7 %collective-permute-start.4 = (f32[4,16,128]{2,1,0:T(8,128)S(1)}, f32[4,16,128]{2,1,0:T(8,128)S(1)}, u32[]{:S(2)}, u32[]{:S(2)}) collective-permute-start(f32[4,16,128]{2,1,0:T(8,128)S(1)} %shard_map.77), channel_id=1, source_target_pairs={{0,8},{8,16},{16,24},{24,0},{1,9},{9,17},{17,25},{25,1},{2,10},{10... | collective-permute-start | bytes 98312 | tf_op jit(solution)/shard_map/ppermute | solution.py:331
  23.0 3.8 %collective-permute-start = (f32[8,19,128]{2,1,0:T(8,128)S(1)}, f32[8,19,128]{2,1,0:T(8,128)S(1)}, u32[]{:S(2)}, u32[]{:S(2)}) collective-permute-start(f32[8,19,128]{2,1,0:T(8,128)S(1)} %all-to-all-done.mine), channel_id=1, source_target_pairs={{0,1},{1,0},{2,3},{3,2},{4,5},{5,4},{6,7},{7,6},{8,9},{9,8},{10,11... | collective-permute-start | bytes 233480 | tf_op jit(solution)/shard_map/ppermute | solution.py:349
  44.2 2.7 %collective-permute-start.7 = (f32[1,16,128]{2,1,0:T(8,128)S(1)}, f32[1,16,128]{2,1,0:T(8,128)S(1)}, u32[]{:S(2)}, u32[]{:S(2)}) collective-permute-start(f32[1,16,128]{2,1,0:T(8,128)S(1)} %shard_map.79.mine), channel_id=1, source_target_pairs={{0,1},{1,0},{2,3},{3,2},{4,5},{5,4},{6,7},{7,6},{8,9},{9,8},{10,11... | collective-permute-start | bytes 24584 | tf_op jit(solution)/shard_map/ppermute | solution.py:366

commit v6 on v5

--- a/solution.py
+++ b/solution.py
@@ -64,12 +64,13 @@
             turned[k * 128 : k * 128 + 128, :] = aug[:, k * 128 : k * 128 + 128].T
 
 
+def ring_pos(to, own):
+    step = (to - own + 4) % 4
+    return jnp.where(step == 0, 0, jnp.where(step == 1, 2, jnp.where(step == 2, 3, 1)))
+
+
 def place(k):
-    def pos(to, own):
-        step = (to - own + 4) % 4
-        return jnp.where(step == 0, 0, jnp.where(step == 1, 2, jnp.where(step == 2, 3, 1)))
-
-    return pos(k // 4, lax.axis_index("y")) * 4 + pos(k % 4, lax.axis_index("x"))
+    return ring_pos(k // 4, lax.axis_index("y")) * 4 + (k % 4 ^ lax.axis_index("x"))
 
 
 def fill_src(aug, turned, sall, bias):
@@ -327,9 +328,10 @@
 
 
 def gather_rows(raw, own):
-    for axis in ("x", "y"):
-        moved = [lax.ppermute(raw, axis, [(i, (i + by) % 4) for i in range(4)]) for by in (1, 3, 2)]
-        raw = own = join([own, *moved], 10**11) if axis == "x" else jnp.concatenate([own, *moved], 0)
+    raw = own = join([own, lax.ppermute(raw, "x", [(i, i ^ 1) for i in range(4)])], 10**6)
+    raw = own = join([own, lax.ppermute(raw, "x", [(i, i ^ 2) for i in range(4)])], 10**11)
+    moved = [lax.ppermute(raw, "y", [(i, (i + by) % 4) for i in range(4)]) for by in (1, 3, 2)]
+    raw = own = jnp.concatenate([own, *moved], 0)
     return own
 
 

time: 73.1 us -> 72.6 us (level)
  blocking collectives: 33.8 us -> 32.8 us
    all_to_all x3, blocking collectives: 33.8 us -> 32.8 us  [exchange(): return lax.all_to_all(v, axes, 0, 0, tiled=True)]
    ppermute x6 -> x5, starting transfers between devices: 9.59 us -> 9.38 us  [the longest x3 4.47 us: gather_rows(): lax.ppermute(raw, 'y', [(i, (i + by) % 4) for i in range(4)])]
    pallas_call x7 -> x8, Pallas kernels: 10.1 us -> 10.1 us  [call(): pl.pallas_call(body, out_shape=[jax.ShapeDtypeStruct(s, f32) for s in out...]
  transfers between devices with their start and end apart: 9 -> 8, of which waited for: 3 -> 3; matrix products, arithmetic and copies ran while one was open for 0% -> 0% of each run, Pallas kernels for 2% -> 2%
where the time goes in v6:
time: 72.6 us; the launch traced here: 71.4 us
  blocking collectives  32.8 us (45%)
  starting transfers between devices  23 us (32%)
  Pallas kernels  10.1 us (14%)
  waiting for transfers between devices  4.85 us (7%)
    all_to_all x3, blocking collectives, exchange(): return lax.all_to_all(v, axes, 0, 0, tiled=True)  32.8 us
    pallas_call x8, Pallas kernels, call(): pl.pallas_call(body, out_shape=[jax.ShapeDtypeStruct(s, f32) for s in out...  10.1 us
    all_to_all x1, starting transfers between devices, exchange(): return lax.all_to_all(v, axes, 0, 0, tiled=True)  8.19 us
    ppermute x3, starting transfers between devices, gather_rows(): lax.ppermute(raw, 'y', [(i, (i + by) % 4) for i in range(4)])  4.47 us
    ppermute x1, starting transfers between devices, local(): other = lax.ppermute(mine, 'c', [(0, 1), (1, 0)])  3.53 us
    all_to_all x1, waiting for transfers between devices, exchange(): return lax.all_to_all(v, axes, 0, 0, tiled=True)  3.09 us
    ppermute x1, starting transfers between devices, gather_rows(): lax.ppermute(raw, 'x', [(i, i ^ 2) for i in range(4)])  2.78 us
    ppermute x1, starting transfers between devices, gather_rows(): lax.ppermute(raw, 'x', [(i, i ^ 1) for i in range(4)])  2.13 us
  transfers between devices with their start and end apart: 8, of which 3 were waited for; matrix products, arithmetic and copies ran while one was open for 0% of the time, Pallas kernels for 2%

profile of v6, /device:TPU:1, one launch (start us, length us, event | category | flops | bytes accessed | tf_op | source)
XLA Modules:
  0.0 71.4 jit_solution(10781918976084921958)
XLA Ops:
  0.6 2.1 %collective-permute-start.1 = (f32[1,16,128]{2,1,0:T(8,128)}, f32[1,16,128]{2,1,0:T(8,128)S(1)}, u32[]{:S(2)}, u32[]{:S(2)}) collective-permute-start(f32[1,16,128]{2,1,0:T(8,128)} %bitcast.6), channel_id=1, source_target_pairs={{0,2},{2,0},{4,6},{6,4},{1,3},{3,1},{5,7},{7,5},{8,10},{10,8},{12,... | collective-permute-start | bytes 24584 | tf_op jit(solution)/shard_map/ppermute | solution.py:331
  2.8 1.4 %shard_map.76 = (f32[8,19,128]{2,1,0:T(8,128)}, f32[1,16,128]{2,1,0:T(8,128)S(1)}, f32[1,128]{1,0:T(1,128)S(1)}) custom-call(f32[16,128]{1,0:T(8,128)} %refs_0_.1, f32[1,128]{1,0:T(1,128)} %bitcast.8, f32[16,128]{1,0:T(8,128)} %refs_2_.1, f32[1,128]{1,0:T(1,128)} %bitcast.9, f32[8,128]{1,0:T(8,128)} %bitcast.7), custom_call_target="tpu_custom_call" | custom-call | tf_op jit(solution)/shard_map/pallas_call | solution.py:303
  4.2 0.0 collective-permute-done.1.refs_1_
  4.2 2.8 %collective-permute-start.2 = (f32[2,16,128]{2,1,0:T(8,128)S(1)}, f32[2,16,128]{2,1,0:T(8,128)S(1)}, u32[]{:S(2)}, u32[]{:S(2)}) collective-permute-start(f32[2,16,128]{2,1,0:T(8,128)S(1)} %shard_map.77.refs_0_), channel_id=1, source_target_pairs={{0,4},{2,6},{4,0},{6,2},{1,5},{3,7},{5,1},{7,3},{8,12},{10,14},{12... | collective-permute-start | bytes 49160 | tf_op jit(solution)/shard_map/ppermute | solution.py:332
  7.0 8.2 %all-to-all-start = ((f32[8,19,128]{2,1,0:T(8,128)}), f32[8,19,128]{2,1,0:T(8,128)S(1)}, u32[]{:S(2)}, u32[]{:S(2)}) async-start(f32[8,19,128]{2,1,0:T(8,128)} %get-tuple-element.14), calls=%async_computation | async-start | bytes 196608 | tf_op jit(solution)/shard_map/all_to_all | solution.py:315
  15.2 0.0 collective-permute-done.2.refs_1_
  15.2 3.0 %collective-permute-start.5 = (f32[4,16,128]{2,1,0:T(8,128)S(1)}, f32[4,16,128]{2,1,0:T(8,128)S(1)}, u32[]{:S(2)}, u32[]{:S(2)}) collective-permute-start(f32[4,16,128]{2,1,0:T(8,128)S(1)} %shard_map.78), channel_id=1, source_target_pairs={{0,16},{8,24},{16,0},{24,8},{1,17},{9,25},{17,1},{25,9},{2,18},{10... | collective-permute-start | bytes 98312 | tf_op jit(solution)/shard_map/ppermute | solution.py:333
  18.2 0.8 %collective-permute-start.4 = (f32[4,16,128]{2,1,0:T(8,128)S(1)}, f32[4,16,128]{2,1,0:T(8,128)S(1)}, u32[]{:S(2)}, u32[]{:S(2)}) collective-permute-start(f32[4,16,128]{2,1,0:T(8,128)S(1)} %shard_map.78), channel_id=1, source_target_pairs={{0,24},{8,0},{16,8},{24,16},{1,25},{9,1},{17,9},{25,17},{2,26},{10... | collective-permute-start | bytes 98312 | tf_op jit(solution)/shard_map/ppermute | solution.py:333
  19.0 0.7 collective-permute-start.3
  19.7 3.1 %all-to-all-done.mine = f32[8,19,128]{2,1,0:T(8,128)S(1)} async-done(((f32[8,19,128]{2,1,0:T(8,128)}), f32[8,19,128]{2,1,0:T(8,128)S(1)}, u32[]{:S(2)}, u32[]{:S(2)}) %all-to-all-start) | async-done | bytes 77856 | tf_op jit(solution)/shard_map/all_to_all | solution.py:315
  22.8 3.5 %collective-permute-start = (f32[8,19,128]{2,1,0:T(8,128)S(1)}, f32[8,19,128]{2,1,0:T(8,128)S(1)}, u32[]{:S(2)}, u32[]{:S(2)}) collective-permute-start(f32[8,19,128]{2,1,0:T(8,128)S(1)} %all-to-all-done.mine), channel_id=1, source_target_pairs={{0,1},{1,0},{2,3},{3,2},{4,5},{5,4},{6,7},{7,6},{8,9},{9,8},{10,11... | collective-permute-start | bytes 233480 | tf_op jit(solution)/shard_map/ppermute | solution.py:351
  26.3 0.0 collective-permute-done.5
  26.3 0.0 collective-permute-done.4
  26.3 0.0 collective-permute-done.3
  26.3 0.9 %collective-permute-done.other = f32[8,19,128]{2,1,0:T(8,128)S(1)} collective-permute-done((f32[8,19,128]{2,1,0:T(8,128)S(1)}, f32[8,19,128]{2,1,0:T(8,128)S(1)}, u32[]{:S(2)}, u32[]{:S(2)}) %collective-permute-start) | collective-permute-done | bytes 77856 | tf_op jit(solution)/shard_map/ppermute | solution.py:351
  27.3 2.9 %shard_map.79 = (f32[16,17,128]{2,1,0:T(8,128)S(1)}, f32[2048,2048]{1,0:T(8,128)S(1)}, f32[16,128]{1,0:T(8,128)S(1)}) custom-call(f32[8,19,128]{2,1,0:T(8,128)S(1)} %all-to-all-done.mine, f32[8,19,128]{2,1,0:T(8,128)S(1)} %collective-permute-done.other, f32[16,16,128]{2,1,0:T(8,128)S(1)} %pad_maximum_fusion.sall, f32[1,128]{1,0:T(1,128)S(1)} %get-tuple-element.16.mass), custom_call_target="tpu_custom_call" | custom-call | tf_op jit(solution)/shard_map/pallas_call | solution.py:303
  30.1 11.9 %all_to_all.20.part = f32[16,17,128]{2,1,0:T(8,128)S(1)} all-to-all(f32[16,17,128]{2,1,0:T(8,128)S(1)} %get-tuple-element.17), channel_id=1, replica_groups=mesh['z'=8,'y'=4,'x'=4,'c'=2] {'y','x'}, dimensions={0} | all-to-all | bytes 278528 | tf_op jit(solution)/shard_map/all_to_all | solution.py:315
  42.0 1.4 %shard_map.80.mine = f32[1,16,128]{2,1,0:T(8,128)S(1)} custom-call(f32[16,17,128]{2,1,0:T(8,128)S(1)} %all_to_all.20.part, f32[2048,2048]{1,0:T(8,128)S(1)} %get-tuple-element.18.kept, f32[16,128]{1,0:T(8,128)S(1)} %get-tuple-element.19.tops, f32[8,19,128]{2,1,0:T(8,128)S(1)} %all-to-all-done.mine, f32[8,19,128]{2,1,0:T(8,128)S(1)} %collective-permute-done.other, ...), custom_call_target="tpu_custom_call" | custom-call | tf_op jit(solution)/shard_map/pallas_call | solution.py:303
  43.4 1.9 %collective-permute-start.6 = (f32[1,16,128]{2,1,0:T(8,128)S(1)}, f32[1,16,128]{2,1,0:T(8,128)S(1)}, u32[]{:S(2)}, u32[]{:S(2)}) collective-permute-start(f32[1,16,128]{2,1,0:T(8,128)S(1)} %shard_map.80.mine), channel_id=1, source_target_pairs={{0,1},{1,0},{2,3},{3,2},{4,5},{5,4},{6,7},{7,6},{8,9},{9,8},{10,11... | collective-permute-start | bytes 24584 | tf_op jit(solution)/shard_map/ppermute | solution.py:368
  45.2 0.8 %collective-permute-done.6.other = f32[1,16,128]{2,1,0:T(8,128)S(1)} collective-permute-done((f32[1,16,128]{2,1,0:T(8,128)S(1)}, f32[1,16,128]{2,1,0:T(8,128)S(1)}, u32[]{:S(2)}, u32[]{:S(2)}) %collective-permute-start.6) | collective-permute-done | bytes 8224 | tf_op jit(solution)/shard_map/ppermute | solution.py:368
  46.1 11.1 %all_to_all.21.part = f32[8,16,128]{2,1,0:T(8,128)S(1)} all-to-all(f32[8,16,128]{2,1,0:T(8,128)S(1)} %shard_map.81), channel_id=1, replica_groups=mesh['z'=8,'y'=4,'x'=4,'c'=2] {'z'}, dimensions={0} | all-to-all | bytes 131072 | tf_op jit(solution)/shard_map/all_to_all | solution.py:315
  57.2 3.7 %shard_map.82 = (f32[16,19,128]{2,1,0:T(8,128)S(1)}, f32[8,128]{1,0:T(8,128)S(1)}) custom-call(f32[8,16,128]{2,1,0:T(8,128)S(1)} %all_to_all.21.part, f32[2048,2048]{1,0:T(8,128)S(1)} %get-tuple-element.18.kept, f32[16,128]{1,0:T(8,128)S(1)} %get-tuple-element.19.tops, f32[8,19,128]{2,1,0:T(8,128)S(1)} %all-to-all-done.mine, ...), custom_call_target="tpu_custom_call" | custom-call | tf_op jit(solution)/shard_map/pallas_call | solution.py:303
  60.8 9.9 %all_to_all.22.part = f32[16,19,128]{2,1,0:T(8,128)S(1)} all-to-all(f32[16,19,128]{2,1,0:T(8,128)S(1)} %get-tuple-element.20), channel_id=1, replica_groups=mesh['z'=8,'y'=4,'x'=4,'c'=2] {'y','x'}, dimensions={0} | all-to-all | bytes 311296 | tf_op jit(solution)/shard_map/all_to_all | solution.py:315
  70.7 0.7 shard_map.83
  (4 shorter events, 0.0 us)
Async XLA Ops:
  0.6 3.6 %collective-permute-start.1 = (f32[1,16,128]{2,1,0:T(8,128)}, f32[1,16,128]{2,1,0:T(8,128)S(1)}, u32[]{:S(2)}, u32[]{:S(2)}) collective-permute-start(f32[1,16,128]{2,1,0:T(8,128)} %bitcast.6), channel_id=1, source_target_pairs={{0,2},{2,0},{4,6},{6,4},{1,3},{3,1},{5,7},{7,5},{8,10},{10,8},{12,... | collective-permute-start | bytes 24584 | tf_op jit(solution)/shard_map/ppermute | solution.py:331
  4.2 11.0 %collective-permute-start.2 = (f32[2,16,128]{2,1,0:T(8,128)S(1)}, f32[2,16,128]{2,1,0:T(8,128)S(1)}, u32[]{:S(2)}, u32[]{:S(2)}) collective-permute-start(f32[2,16,128]{2,1,0:T(8,128)S(1)} %shard_map.77.refs_0_), channel_id=1, source_target_pairs={{0,4},{2,6},{4,0},{6,2},{1,5},{3,7},{5,1},{7,3},{8,12},{10,14},{12... | collective-permute-start | bytes 49160 | tf_op jit(solution)/shard_map/ppermute | solution.py:332
  7.0 15.8 %all-to-all-start = ((f32[8,19,128]{2,1,0:T(8,128)}), f32[8,19,128]{2,1,0:T(8,128)S(1)}, u32[]{:S(2)}, u32[]{:S(2)}) async-start(f32[8,19,128]{2,1,0:T(8,128)} %get-tuple-element.14), calls=%async_computation | async-start | bytes 196608 | tf_op jit(solution)/shard_map/all_to_all | solution.py:315
  15.2 11.1 %collective-permute-start.5 = (f32[4,16,128]{2,1,0:T(8,128)S(1)}, f32[4,16,128]{2,1,0:T(8,128)S(1)}, u32[]{:S(2)}, u32[]{:S(2)}) collective-permute-start(f32[4,16,128]{2,1,0:T(8,128)S(1)} %shard_map.78), channel_id=1, source_target_pairs={{0,16},{8,24},{16,0},{24,8},{1,17},{9,25},{17,1},{25,9},{2,18},{10... | collective-permute-start | bytes 98312 | tf_op jit(solution)/shard_map/ppermute | solution.py:333
  18.2 8.1 %collective-permute-start.4 = (f32[4,16,128]{2,1,0:T(8,128)S(1)}, f32[4,16,128]{2,1,0:T(8,128)S(1)}, u32[]{:S(2)}, u32[]{:S(2)}) collective-permute-start(f32[4,16,128]{2,1,0:T(8,128)S(1)} %shard_map.78), channel_id=1, source_target_pairs={{0,24},{8,0},{16,8},{24,16},{1,25},{9,1},{17,9},{25,17},{2,26},{10... | collective-permute-start | bytes 98312 | tf_op jit(solution)/shard_map/ppermute | solution.py:333
  19.0 7.3 %collective-permute-start.3 = (f32[4,16,128]{2,1,0:T(8,128)S(1)}, f32[4,16,128]{2,1,0:T(8,128)S(1)}, u32[]{:S(2)}, u32[]{:S(2)}) collective-permute-start(f32[4,16,128]{2,1,0:T(8,128)S(1)} %shard_map.78), channel_id=1, source_target_pairs={{0,8},{8,16},{16,24},{24,0},{1,9},{9,17},{17,25},{25,1},{2,10},{10... | collective-permute-start | bytes 98312 | tf_op jit(solution)/shard_map/ppermute | solution.py:333
  22.8 4.5 %collective-permute-start = (f32[8,19,128]{2,1,0:T(8,128)S(1)}, f32[8,19,128]{2,1,0:T(8,128)S(1)}, u32[]{:S(2)}, u32[]{:S(2)}) collective-permute-start(f32[8,19,128]{2,1,0:T(8,128)S(1)} %all-to-all-done.mine), channel_id=1, source_target_pairs={{0,1},{1,0},{2,3},{3,2},{4,5},{5,4},{6,7},{7,6},{8,9},{9,8},{10,11... | collective-permute-start | bytes 233480 | tf_op jit(solution)/shard_map/ppermute | solution.py:351
  43.4 2.7 %collective-permute-start.6 = (f32[1,16,128]{2,1,0:T(8,128)S(1)}, f32[1,16,128]{2,1,0:T(8,128)S(1)}, u32[]{:S(2)}, u32[]{:S(2)}) collective-permute-start(f32[1,16,128]{2,1,0:T(8,128)S(1)} %shard_map.80.mine), channel_id=1, source_target_pairs={{0,1},{1,0},{2,3},{3,2},{4,5},{5,4},{6,7},{7,6},{8,9},{9,8},{10,11... | collective-permute-start | bytes 24584 | tf_op jit(solution)/shard_map/ppermute | solution.py:368

commit v7 on v6

--- a/solution.py
+++ b/solution.py
@@ -171,14 +171,17 @@
         tops[pl.ds(2 * c, 1), :] = top[:, :128]
         tops[pl.ds(2 * c + 1, 1), :] = top[:, 128:]
 
-    blocks, groups = saug.shape[1] // 256, tturn.shape[0] // 256
-    shifts = [sample_top(tturn, saug[:, c * 256 : c * 256 + 256], groups) for c in range(blocks)]
-    ok = jnp.ones((1, 256), f32)
-    for c in range(blocks):
-        e = jnp.exp2(scores(tturn[...], saug[:, c * 256 : c * 256 + 256]) - shifts[c])
-        kept[:, c * 256 : c * 256 + 256] = e
-        s = jnp.sum(jnp.sum(e.reshape(e.shape[0] // 8, 8, 256), 0), 0, keepdims=True)
-        put(c, shifts[c] + jnp.log2(s), shifts[c])
+    width, groups = 1024, tturn.shape[0] // 256
+    blocks = [slice(at, at + width) for at in range(0, saug.shape[1], width)]
+    shifts = [sample_top(tturn, saug[:, cols], groups) for cols in blocks]
+    ok = jnp.ones((1, width), f32)
+    for cols, shift in zip(blocks, shifts):
+        e = jnp.exp2(scores(tturn[...], saug[:, cols]) - shift)
+        kept[:, cols] = e
+        s = jnp.sum(jnp.sum(e.reshape(e.shape[0] // 8, 8, width), 0), 0, keepdims=True)
+        line = shift + jnp.log2(s)
+        for at in range(0, width, 256):
+            put((cols.start + at) // 256, line[:, at : at + 256], shift[:, at : at + 256])
         ok = jnp.minimum(ok, jnp.where(s < 2.0**40, 1.0, 0.0))
 
     @pl.when(jnp.min(ok) < 0.5)

time: 72.6 us -> 72.6 us (level)
  no operation moved by 1% of the time
where the time goes in v7:
time: 72.6 us; the launch traced here: 71.4 us
  blocking collectives  32.9 us (45%)
  starting transfers between devices  23 us (32%)
  Pallas kernels  10 us (14%)
  waiting for transfers between devices  4.85 us (7%)
    all_to_all x3, blocking collectives, exchange(): return lax.all_to_all(v, axes, 0, 0, tiled=True)  32.9 us
    pallas_call x8, Pallas kernels, call(): pl.pallas_call(body, out_shape=[jax.ShapeDtypeStruct(s, f32) for s in out...  10 us
    all_to_all x1, starting transfers between devices, exchange(): return lax.all_to_all(v, axes, 0, 0, tiled=True)  8.19 us
    ppermute x3, starting transfers between devices, gather_rows(): lax.ppermute(raw, 'y', [(i, (i + by) % 4) for i in range(4)])  4.47 us
    ppermute x1, starting transfers between devices, local(): other = lax.ppermute(mine, 'c', [(0, 1), (1, 0)])  3.53 us
    all_to_all x1, waiting for transfers between devices, exchange(): return lax.all_to_all(v, axes, 0, 0, tiled=True)  3.09 us
    ppermute x1, starting transfers between devices, gather_rows(): lax.ppermute(raw, 'x', [(i, i ^ 2) for i in range(4)])  2.78 us
    ppermute x1, starting transfers between devices, gather_rows(): lax.ppermute(raw, 'x', [(i, i ^ 1) for i in range(4)])  2.13 us
  transfers between devices with their start and end apart: 8, of which 3 were waited for; matrix products, arithmetic and copies ran while one was open for 0% of the time, Pallas kernels for 2%

profile of v7, /device:TPU:1, one launch (start us, length us, event | category | flops | bytes accessed | tf_op | source)
XLA Modules:
  0.0 71.4 jit_solution(9583994112050312514)
XLA Ops:
  0.6 2.1 %collective-permute-start.1 = (f32[1,16,128]{2,1,0:T(8,128)}, f32[1,16,128]{2,1,0:T(8,128)S(1)}, u32[]{:S(2)}, u32[]{:S(2)}) collective-permute-start(f32[1,16,128]{2,1,0:T(8,128)} %bitcast.6), channel_id=1, source_target_pairs={{0,2},{2,0},{4,6},{6,4},{1,3},{3,1},{5,7},{7,5},{8,10},{10,8},{12,... | collective-permute-start | bytes 24584 | tf_op jit(solution)/shard_map/ppermute | solution.py:334
  2.8 1.4 %shard_map.76 = (f32[8,19,128]{2,1,0:T(8,128)}, f32[1,16,128]{2,1,0:T(8,128)S(1)}, f32[1,128]{1,0:T(1,128)S(1)}) custom-call(f32[16,128]{1,0:T(8,128)} %refs_0_.1, f32[1,128]{1,0:T(1,128)} %bitcast.8, f32[16,128]{1,0:T(8,128)} %refs_2_.1, f32[1,128]{1,0:T(1,128)} %bitcast.9, f32[8,128]{1,0:T(8,128)} %bitcast.7), custom_call_target="tpu_custom_call" | custom-call | tf_op jit(solution)/shard_map/pallas_call | solution.py:306
  4.2 0.0 collective-permute-done.1.refs_1_
  4.2 2.8 %collective-permute-start.2 = (f32[2,16,128]{2,1,0:T(8,128)S(1)}, f32[2,16,128]{2,1,0:T(8,128)S(1)}, u32[]{:S(2)}, u32[]{:S(2)}) collective-permute-start(f32[2,16,128]{2,1,0:T(8,128)S(1)} %shard_map.77.refs_0_), channel_id=1, source_target_pairs={{0,4},{2,6},{4,0},{6,2},{1,5},{3,7},{5,1},{7,3},{8,12},{10,14},{12... | collective-permute-start | bytes 49160 | tf_op jit(solution)/shard_map/ppermute | solution.py:335
  7.0 8.2 %all-to-all-start = ((f32[8,19,128]{2,1,0:T(8,128)}), f32[8,19,128]{2,1,0:T(8,128)S(1)}, u32[]{:S(2)}, u32[]{:S(2)}) async-start(f32[8,19,128]{2,1,0:T(8,128)} %get-tuple-element.14), calls=%async_computation | async-start | bytes 196608 | tf_op jit(solution)/shard_map/all_to_all | solution.py:318
  15.2 0.0 collective-permute-done.2.refs_1_
  15.2 3.0 %collective-permute-start.5 = (f32[4,16,128]{2,1,0:T(8,128)S(1)}, f32[4,16,128]{2,1,0:T(8,128)S(1)}, u32[]{:S(2)}, u32[]{:S(2)}) collective-permute-start(f32[4,16,128]{2,1,0:T(8,128)S(1)} %shard_map.78), channel_id=1, source_target_pairs={{0,16},{8,24},{16,0},{24,8},{1,17},{9,25},{17,1},{25,9},{2,18},{10... | collective-permute-start | bytes 98312 | tf_op jit(solution)/shard_map/ppermute | solution.py:336
  18.2 0.8 %collective-permute-start.4 = (f32[4,16,128]{2,1,0:T(8,128)S(1)}, f32[4,16,128]{2,1,0:T(8,128)S(1)}, u32[]{:S(2)}, u32[]{:S(2)}) collective-permute-start(f32[4,16,128]{2,1,0:T(8,128)S(1)} %shard_map.78), channel_id=1, source_target_pairs={{0,24},{8,0},{16,8},{24,16},{1,25},{9,1},{17,9},{25,17},{2,26},{10... | collective-permute-start | bytes 98312 | tf_op jit(solution)/shard_map/ppermute | solution.py:336
  19.0 0.7 collective-permute-start.3
  19.7 3.1 %all-to-all-done.mine = f32[8,19,128]{2,1,0:T(8,128)S(1)} async-done(((f32[8,19,128]{2,1,0:T(8,128)}), f32[8,19,128]{2,1,0:T(8,128)S(1)}, u32[]{:S(2)}, u32[]{:S(2)}) %all-to-all-start) | async-done | bytes 77856 | tf_op jit(solution)/shard_map/all_to_all | solution.py:318
  22.8 3.5 %collective-permute-start = (f32[8,19,128]{2,1,0:T(8,128)S(1)}, f32[8,19,128]{2,1,0:T(8,128)S(1)}, u32[]{:S(2)}, u32[]{:S(2)}) collective-permute-start(f32[8,19,128]{2,1,0:T(8,128)S(1)} %all-to-all-done.mine), channel_id=1, source_target_pairs={{0,1},{1,0},{2,3},{3,2},{4,5},{5,4},{6,7},{7,6},{8,9},{9,8},{10,11... | collective-permute-start | bytes 233480 | tf_op jit(solution)/shard_map/ppermute | solution.py:354
  26.3 0.0 collective-permute-done.5
  26.3 0.0 collective-permute-done.4
  26.3 0.0 collective-permute-done.3
  26.3 0.9 %collective-permute-done.other = f32[8,19,128]{2,1,0:T(8,128)S(1)} collective-permute-done((f32[8,19,128]{2,1,0:T(8,128)S(1)}, f32[8,19,128]{2,1,0:T(8,128)S(1)}, u32[]{:S(2)}, u32[]{:S(2)}) %collective-permute-start) | collective-permute-done | bytes 77856 | tf_op jit(solution)/shard_map/ppermute | solution.py:354
  27.3 2.9 %shard_map.79 = (f32[16,17,128]{2,1,0:T(8,128)S(1)}, f32[2048,2048]{1,0:T(8,128)S(1)}, f32[16,128]{1,0:T(8,128)S(1)}) custom-call(f32[8,19,128]{2,1,0:T(8,128)S(1)} %all-to-all-done.mine, f32[8,19,128]{2,1,0:T(8,128)S(1)} %collective-permute-done.other, f32[16,16,128]{2,1,0:T(8,128)S(1)} %pad_maximum_fusion.sall, f32[1,128]{1,0:T(1,128)S(1)} %get-tuple-element.16.mass), custom_call_target="tpu_custom_call" | custom-call | tf_op jit(solution)/shard_map/pallas_call | solution.py:306
  30.1 11.9 %all_to_all.20.part = f32[16,17,128]{2,1,0:T(8,128)S(1)} all-to-all(f32[16,17,128]{2,1,0:T(8,128)S(1)} %get-tuple-element.17), channel_id=1, replica_groups=mesh['z'=8,'y'=4,'x'=4,'c'=2] {'y','x'}, dimensions={0} | all-to-all | bytes 278528 | tf_op jit(solution)/shard_map/all_to_all | solution.py:318
  42.0 1.4 %shard_map.80.mine = f32[1,16,128]{2,1,0:T(8,128)S(1)} custom-call(f32[16,17,128]{2,1,0:T(8,128)S(1)} %all_to_all.20.part, f32[2048,2048]{1,0:T(8,128)S(1)} %get-tuple-element.18.kept, f32[16,128]{1,0:T(8,128)S(1)} %get-tuple-element.19.tops, f32[8,19,128]{2,1,0:T(8,128)S(1)} %all-to-all-done.mine, f32[8,19,128]{2,1,0:T(8,128)S(1)} %collective-permute-done.other, ...), custom_call_target="tpu_custom_call" | custom-call | tf_op jit(solution)/shard_map/pallas_call | solution.py:306
  43.4 1.9 %collective-permute-start.6 = (f32[1,16,128]{2,1,0:T(8,128)S(1)}, f32[1,16,128]{2,1,0:T(8,128)S(1)}, u32[]{:S(2)}, u32[]{:S(2)}) collective-permute-start(f32[1,16,128]{2,1,0:T(8,128)S(1)} %shard_map.80.mine), channel_id=1, source_target_pairs={{0,1},{1,0},{2,3},{3,2},{4,5},{5,4},{6,7},{7,6},{8,9},{9,8},{10,11... | collective-permute-start | bytes 24584 | tf_op jit(solution)/shard_map/ppermute | solution.py:371
  45.2 0.8 %collective-permute-done.6.other = f32[1,16,128]{2,1,0:T(8,128)S(1)} collective-permute-done((f32[1,16,128]{2,1,0:T(8,128)S(1)}, f32[1,16,128]{2,1,0:T(8,128)S(1)}, u32[]{:S(2)}, u32[]{:S(2)}) %collective-permute-start.6) | collective-permute-done | bytes 8224 | tf_op jit(solution)/shard_map/ppermute | solution.py:371
  46.1 11.1 %all_to_all.21.part = f32[8,16,128]{2,1,0:T(8,128)S(1)} all-to-all(f32[8,16,128]{2,1,0:T(8,128)S(1)} %shard_map.81), channel_id=1, replica_groups=mesh['z'=8,'y'=4,'x'=4,'c'=2] {'z'}, dimensions={0} | all-to-all | bytes 131072 | tf_op jit(solution)/shard_map/all_to_all | solution.py:318
  57.1 3.7 %shard_map.82 = (f32[16,19,128]{2,1,0:T(8,128)S(1)}, f32[8,128]{1,0:T(8,128)S(1)}) custom-call(f32[8,16,128]{2,1,0:T(8,128)S(1)} %all_to_all.21.part, f32[2048,2048]{1,0:T(8,128)S(1)} %get-tuple-element.18.kept, f32[16,128]{1,0:T(8,128)S(1)} %get-tuple-element.19.tops, f32[8,19,128]{2,1,0:T(8,128)S(1)} %all-to-all-done.mine, ...), custom_call_target="tpu_custom_call" | custom-call | tf_op jit(solution)/shard_map/pallas_call | solution.py:306
  60.8 9.9 %all_to_all.22.part = f32[16,19,128]{2,1,0:T(8,128)S(1)} all-to-all(f32[16,19,128]{2,1,0:T(8,128)S(1)} %get-tuple-element.20), channel_id=1, replica_groups=mesh['z'=8,'y'=4,'x'=4,'c'=2] {'y','x'}, dimensions={0} | all-to-all | bytes 311296 | tf_op jit(solution)/shard_map/all_to_all | solution.py:318
  70.7 0.7 shard_map.83
  (4 shorter events, 0.0 us)
Async XLA Ops:
  0.6 3.6 %collective-permute-start.1 = (f32[1,16,128]{2,1,0:T(8,128)}, f32[1,16,128]{2,1,0:T(8,128)S(1)}, u32[]{:S(2)}, u32[]{:S(2)}) collective-permute-start(f32[1,16,128]{2,1,0:T(8,128)} %bitcast.6), channel_id=1, source_target_pairs={{0,2},{2,0},{4,6},{6,4},{1,3},{3,1},{5,7},{7,5},{8,10},{10,8},{12,... | collective-permute-start | bytes 24584 | tf_op jit(solution)/shard_map/ppermute | solution.py:334
  4.2 11.0 %collective-permute-start.2 = (f32[2,16,128]{2,1,0:T(8,128)S(1)}, f32[2,16,128]{2,1,0:T(8,128)S(1)}, u32[]{:S(2)}, u32[]{:S(2)}) collective-permute-start(f32[2,16,128]{2,1,0:T(8,128)S(1)} %shard_map.77.refs_0_), channel_id=1, source_target_pairs={{0,4},{2,6},{4,0},{6,2},{1,5},{3,7},{5,1},{7,3},{8,12},{10,14},{12... | collective-permute-start | bytes 49160 | tf_op jit(solution)/shard_map/ppermute | solution.py:335
  7.0 15.8 %all-to-all-start = ((f32[8,19,128]{2,1,0:T(8,128)}), f32[8,19,128]{2,1,0:T(8,128)S(1)}, u32[]{:S(2)}, u32[]{:S(2)}) async-start(f32[8,19,128]{2,1,0:T(8,128)} %get-tuple-element.14), calls=%async_computation | async-start | bytes 196608 | tf_op jit(solution)/shard_map/all_to_all | solution.py:318
  15.2 11.1 %collective-permute-start.5 = (f32[4,16,128]{2,1,0:T(8,128)S(1)}, f32[4,16,128]{2,1,0:T(8,128)S(1)}, u32[]{:S(2)}, u32[]{:S(2)}) collective-permute-start(f32[4,16,128]{2,1,0:T(8,128)S(1)} %shard_map.78), channel_id=1, source_target_pairs={{0,16},{8,24},{16,0},{24,8},{1,17},{9,25},{17,1},{25,9},{2,18},{10... | collective-permute-start | bytes 98312 | tf_op jit(solution)/shard_map/ppermute | solution.py:336
  18.2 8.1 %collective-permute-start.4 = (f32[4,16,128]{2,1,0:T(8,128)S(1)}, f32[4,16,128]{2,1,0:T(8,128)S(1)}, u32[]{:S(2)}, u32[]{:S(2)}) collective-permute-start(f32[4,16,128]{2,1,0:T(8,128)S(1)} %shard_map.78), channel_id=1, source_target_pairs={{0,24},{8,0},{16,8},{24,16},{1,25},{9,1},{17,9},{25,17},{2,26},{10... | collective-permute-start | bytes 98312 | tf_op jit(solution)/shard_map/ppermute | solution.py:336
  19.0 7.3 %collective-permute-start.3 = (f32[4,16,128]{2,1,0:T(8,128)S(1)}, f32[4,16,128]{2,1,0:T(8,128)S(1)}, u32[]{:S(2)}, u32[]{:S(2)}) collective-permute-start(f32[4,16,128]{2,1,0:T(8,128)S(1)} %shard_map.78), channel_id=1, source_target_pairs={{0,8},{8,16},{16,24},{24,0},{1,9},{9,17},{17,25},{25,1},{2,10},{10... | collective-permute-start | bytes 98312 | tf_op jit(solution)/shard_map/ppermute | solution.py:336
  22.8 4.5 %collective-permute-start = (f32[8,19,128]{2,1,0:T(8,128)S(1)}, f32[8,19,128]{2,1,0:T(8,128)S(1)}, u32[]{:S(2)}, u32[]{:S(2)}) collective-permute-start(f32[8,19,128]{2,1,0:T(8,128)S(1)} %all-to-all-done.mine), channel_id=1, source_target_pairs={{0,1},{1,0},{2,3},{3,2},{4,5},{5,4},{6,7},{7,6},{8,9},{9,8},{10,11... | collective-permute-start | bytes 233480 | tf_op jit(solution)/shard_map/ppermute | solution.py:354
  43.4 2.7 %collective-permute-start.6 = (f32[1,16,128]{2,1,0:T(8,128)S(1)}, f32[1,16,128]{2,1,0:T(8,128)S(1)}, u32[]{:S(2)}, u32[]{:S(2)}) collective-permute-start(f32[1,16,128]{2,1,0:T(8,128)S(1)} %shard_map.80.mine), channel_id=1, source_target_pairs={{0,1},{1,0},{2,3},{3,2},{4,5},{5,4},{6,7},{7,6},{8,9},{9,8},{10,11... | collective-permute-start | bytes 24584 | tf_op jit(solution)/shard_map/ppermute | solution.py:371
